TPU v7x, 128 devices: a whole 4x4x4 slice. The times are simulated.
128 devices in a mesh: pix: 32 (over z, x, core), beam: 4 (over y).
Axes of the slice: x: 4, y: 4, z: 4, core: 2. Of those that a mesh axis runs over, the one named last changes fastest.
Arguments:
- sketch: bfloat16 [512, 128, 256], P('beam', 'pix'), may hold values from -6 to 6
- gains: bfloat16 [2048, 32, 128, 128], P('pix', 'beam'), may hold values from -0.09375 to 0.09375
- coverage: int32 [2048, 32], P('pix', 'beam'), may hold values from 0 to 127
Outputs:
- basis: float32 [512, 128, 256], P('beam', 'pix')
- factor: float32 [256, 256], replicated
Inputs may be any that keep to these rules, and one draw needn't show every extreme that they name: `coverage`: entries name beam blocks within the slot's group of 128 blocks; a block may be named by several slots.
All inputs are finite; a program needn't handle non-finite values.
Results may differ from a plain program's by a relative error of at most 0.0011.
Values may be sent and summed in bfloat16 or wider, within the bound.
A program may use at most 192 MiB of HBM per device.

v0:
```python
import math

import jax
import jax.numpy as jnp
from jax import lax
from jax.sharding import PartitionSpec as P

BEAMS = 65536


def local(sketch, gains, coverage):
    tiles_here = gains.shape[0]
    slots_here = gains.shape[1]
    block_size = gains.shape[2]
    width = sketch.shape[2]
    blocks_here = sketch.shape[0]
    group_size = math.gcd(tiles_here, 8)
    group_count = tiles_here // group_size
    grouped_gains = gains.reshape(group_count, group_size, slots_here, block_size, block_size)
    grouped_ids = coverage.reshape(group_count, group_size, slots_here)
    full_sketch = lax.all_gather(sketch, "pix", axis=1, tiled=True)

    def pixel_pass(args):
        tile_gains, tile_ids = args
        picked = full_sketch[tile_ids]
        return jnp.einsum("tsab,tsbk->tak", tile_gains, picked, preferred_element_type=jnp.float32)

    partial_sketch = lax.map(pixel_pass, (grouped_gains, grouped_ids)).reshape(
        tiles_here, block_size, width
    )
    rounded = lax.psum(partial_sketch, "beam").astype(jnp.bfloat16)
    grouped_rows = rounded.reshape(group_count, group_size, block_size, width)

    def step(total, args):
        tile_gains, tile_ids, tile_rows = args
        contrib = jnp.einsum(
            "tsab,tak->tsbk", tile_gains, tile_rows, preferred_element_type=jnp.float32
        )
        return (total.at[tile_ids.reshape(-1)].add(contrib.reshape(-1, block_size, width)), None)

    empty = jnp.zeros((blocks_here, block_size, width), jnp.float32)
    total, _ = lax.scan(step, empty, (grouped_gains, grouped_ids, grouped_rows))
    range_rows = lax.psum_scatter(total, "pix", scatter_dimension=1, tiled=True)
    flat = range_rows.reshape(-1, width)
    local_gram = jnp.dot(
        flat.T, flat, precision=lax.Precision.HIGHEST, preferred_element_type=jnp.float32
    )
    gram = lax.psum(local_gram, ("pix", "beam"))
    lower = jnp.linalg.cholesky(gram)
    solved = jax.scipy.linalg.solve_triangular(lower, flat.T, lower=True).T
    scale = jnp.sqrt(jnp.float32(BEAMS))
    return ((solved * scale).reshape(range_rows.shape), lower.T / scale)


def solution(mesh):
    return jax.shard_map(
        local,
        mesh=mesh,
        in_specs=(P("beam", "pix", None), P("pix", "beam", None, None), P("pix", "beam")),
        out_specs=(P("beam", "pix", None), P()),
        check_vma=False,
    )
```

profile of v0, /device:TPU:1, one launch (start us, length us, event | category | flops | bytes accessed | tf_op | source)
XLA Modules:
  0.0 879.5 jit_solution(11138806634660061475)
XLA Ops:
  9.7 22.5 %copy.36 = bf16[64,8,128,128]{2,3,1,0:T(8,128)(2,1)} copy(bf16[64,8,128,128]{3,2,1,0:T(8,128)(2,1)} %param.8) | data formatting | bytes 33554432 | tf_op args[1]
  32.2 35.3 %all-gather.2.cloned.1.call-done = bf16[128,128,256]{2,0,1:T(8,128)(2,1)} async-done(((bf16[128,4,256]{2,0,1:T(8,128)(2,1)}), bf16[128,128,256]{2,0,1:T(8,128)(2,1)}) %all-gather.2.cloned.1.call-update) | async-done | bytes 8388624 | tf_op jit(solution)/shard_map/all_gather | solution.py:21
  67.5 11.4 %copy.39 = bf16[128,128,256]{2,1,0:T(8,128)(2,1)} copy(bf16[128,128,256]{2,0,1:T(8,128)(2,1)} %all-gather.2.cloned.1.call-done) | data formatting | bytes 16777216 | tf_op jit(solution)/shard_map/while | solution.py:28
  78.9 87.8 %while.21 = (s32[]{:T(128)}, f32[8,8,128,256]{3,2,1,0:T(8,128)}, bf16[8,8,8,128,128]{4,3,2,1,0:T(8,128)(2,1)}, s32[8,8,8]{2,1,0:T(8,128)S(1)}, bf16[128,128,256]{2,1,0:T(8,128)(2,1)}, /*index=5*/s32[]{:T(128)}) while((s32[]{:T(128)}, f32[8,8,128,256]{3,2,1,0:T(8,128)}, bf16[8,8,8,128,128]{4,3,2,1,0:T(8,128)(2,1)}, s32[8,8,8]{2,1,0:T(8,128)S(1)}, ...), condition=%wide.region_1.2_spmd, body=%wide.region_0.1_spmd.sunk | while | flops 536872128 | bytes 15735369 | solution.py:28
  79.0 6.2 gather_fusion
  90.0 6.2 gather_fusion
  166.7 148.6 %all-reduce.5 = bf16[64,128,256]{2,1,0:T(8,128)(2,1)} all-reduce(f32[64,128,256]{2,1,0:T(8,128)} %bitcast.99), channel_id=1, replica_groups=mesh['pix'=32,'beam'=4] {'beam'}, use_global_device_ids=true, to_apply=%region_2.3 | all-reduce | flops 2097152 | bytes 12582912 | tf_op jit(solution)/shard_map/psum | solution.py:31
  315.3 7.8 broadcast_in_dim.14
  323.1 206.1 %while.22 = (s32[]{:T(128)}, f32[128,128,256]{2,1,0:T(8,128)}, s32[8,8,8]{2,1,0:T(8,128)S(1)}, bf16[8,8,8,128,128]{3,4,2,1,0:T(8,128)(2,1)}, bf16[8,8,128,256]{3,2,1,0:T(8,128)(2,1)}, /*index=5*/s32[]{:T(128)}) while((s32[]{:T(128)}, f32[128,128,256]{2,1,0:T(8,128)}, s32[8,8,8]{2,1,0:T(8,128)S(1)}, bf16[8,8,8,128,128]{3,4,2,1,0:T(8,128)(2,1)}, ...), condition=%wide.region_5.6_spmd, body=%wide.region_3.5_spmd.sunk | while | flops 538968256 | bytes 36178760 | solution.py:42
  329.3 19.6 %scatter_fusion = f32[128,128,256]{2,1,0:T(8,128)} fusion(f32[128,128,256]{2,1,0:T(8,128)} %get-tuple-element.250, s32[64]{0:T(128)S(1)} %fusion.48, f32[64,128,256]{2,1,0:T(8,128)} %bitcast.94), kind=kCustom, calls=%fused_computation.1.clone.1 | custom fusion | flops 2097152 | bytes 25166080 | tf_op jit(solution)/shard_map/while/body/eval_jaxpr/scatter-add | solution.py:39
  355.1 19.7 %scatter_fusion = f32[128,128,256]{2,1,0:T(8,128)} fusion(f32[128,128,256]{2,1,0:T(8,128)} %get-tuple-element.250, s32[64]{0:T(128)S(1)} %fusion.48, f32[64,128,256]{2,1,0:T(8,128)} %bitcast.94), kind=kCustom, calls=%fused_computation.1.clone.1 | custom fusion | flops 2097152 | bytes 25166080 | tf_op jit(solution)/shard_map/while/body/eval_jaxpr/scatter-add | solution.py:39
  381.0 19.6 %scatter_fusion = f32[128,128,256]{2,1,0:T(8,128)} fusion(f32[128,128,256]{2,1,0:T(8,128)} %get-tuple-element.250, s32[64]{0:T(128)S(1)} %fusion.48, f32[64,128,256]{2,1,0:T(8,128)} %bitcast.94), kind=kCustom, calls=%fused_computation.1.clone.1 | custom fusion | flops 2097152 | bytes 25166080 | tf_op jit(solution)/shard_map/while/body/eval_jaxpr/scatter-add | solution.py:39
  406.9 19.7 %scatter_fusion = f32[128,128,256]{2,1,0:T(8,128)} fusion(f32[128,128,256]{2,1,0:T(8,128)} %get-tuple-element.250, s32[64]{0:T(128)S(1)} %fusion.48, f32[64,128,256]{2,1,0:T(8,128)} %bitcast.94), kind=kCustom, calls=%fused_computation.1.clone.1 | custom fusion | flops 2097152 | bytes 25166080 | tf_op jit(solution)/shard_map/while/body/eval_jaxpr/scatter-add | solution.py:39
  432.8 19.6 %scatter_fusion = f32[128,128,256]{2,1,0:T(8,128)} fusion(f32[128,128,256]{2,1,0:T(8,128)} %get-tuple-element.250, s32[64]{0:T(128)S(1)} %fusion.48, f32[64,128,256]{2,1,0:T(8,128)} %bitcast.94), kind=kCustom, calls=%fused_computation.1.clone.1 | custom fusion | flops 2097152 | bytes 25166080 | tf_op jit(solution)/shard_map/while/body/eval_jaxpr/scatter-add | solution.py:39
  458.5 19.4 %scatter_fusion = f32[128,128,256]{2,1,0:T(8,128)} fusion(f32[128,128,256]{2,1,0:T(8,128)} %get-tuple-element.250, s32[64]{0:T(128)S(1)} %fusion.48, f32[64,128,256]{2,1,0:T(8,128)} %bitcast.94), kind=kCustom, calls=%fused_computation.1.clone.1 | custom fusion | flops 2097152 | bytes 25166080 | tf_op jit(solution)/shard_map/while/body/eval_jaxpr/scatter-add | solution.py:39
  484.1 19.6 %scatter_fusion = f32[128,128,256]{2,1,0:T(8,128)} fusion(f32[128,128,256]{2,1,0:T(8,128)} %get-tuple-element.250, s32[64]{0:T(128)S(1)} %fusion.48, f32[64,128,256]{2,1,0:T(8,128)} %bitcast.94), kind=kCustom, calls=%fused_computation.1.clone.1 | custom fusion | flops 2097152 | bytes 25166080 | tf_op jit(solution)/shard_map/while/body/eval_jaxpr/scatter-add | solution.py:39
  509.9 19.4 %scatter_fusion = f32[128,128,256]{2,1,0:T(8,128)} fusion(f32[128,128,256]{2,1,0:T(8,128)} %get-tuple-element.250, s32[64]{0:T(128)S(1)} %fusion.48, f32[64,128,256]{2,1,0:T(8,128)} %bitcast.94), kind=kCustom, calls=%fused_computation.1.clone.1 | custom fusion | flops 2097152 | bytes 25166080 | tf_op jit(solution)/shard_map/while/body/eval_jaxpr/scatter-add | solution.py:39
  529.3 17.7 %copy.40 = f32[128,128,256]{2,0,1:T(8,128)} copy(f32[128,128,256]{2,1,0:T(8,128)} %get-tuple-element.57) | data formatting | bytes 33554432 | tf_op jit(solution)/shard_map/while | solution.py:42
  547.3 112.8 %reduce-scatter.2.cloned.1.call-done = f32[128,4,256]{2,0,1:T(8,128)} async-done(((f32[128,128,256]{2,0,1:T(8,128)}), f32[128,4,256]{2,0,1:T(8,128)}) %reduce-scatter.2.cloned.1.call-update) | async-done | bytes 524304 | tf_op jit(solution)/shard_map/reduce_scatter | solution.py:43
  664.9 142.7 %all-reduce.4.cloned.1.call-done = f32[256,256]{0,1:T(8,128)} async-done(((f32[256,256]{0,1:T(8,128)}), f32[256,256]{0,1:T(8,128)}) %all-reduce.4.cloned.1.call-update) | async-done | bytes 262160 | tf_op jit(solution)/shard_map/psum | solution.py:48
  809.6 11.7 %cholesky.50 = f32[128,128]{1,0:T(8,128)S(1)} custom-call(f32[128,128]{1,0:T(8,128)S(1)} %cholesky.118), custom_call_target="Cholesky" | custom-call | tf_op jit(solution)/shard_map/jit(cholesky)/cholesky | solution.py:49
  821.4 9.8 %custom-call.15 = f32[1,128,128]{1,2,0:T(8,128)S(1)} custom-call(f32[1,128,128]{2,1,0:T(8,128)S(1)} %get-tuple-element.129), custom_call_target="InvertDiagBlocksLowerTriangular" | custom-call | tf_op jit(solution)/shard_map/jit(cholesky)/cholesky | solution.py:49
  831.7 11.7 %cholesky.105 = f32[128,128]{1,0:T(8,128)S(1)} custom-call(f32[128,128]{1,0:T(8,128)S(1)} %convolution_subtract_fusion.1), custom_call_target="Cholesky" | custom-call | tf_op jit(solution)/shard_map/jit(cholesky)/cholesky | solution.py:49
  850.0 19.7 %custom-call.16 = f32[2,128,128]{1,2,0:T(8,128)S(1)} custom-call(f32[2,128,128]{2,1,0:T(8,128)S(1)} %get-tuple-element.65), custom_call_target="InvertDiagBlocksLowerTriangular" | custom-call | tf_op jit(solution)/shard_map/jit(_solve_triangular)/triangular_solve | solution.py:50
  (110 shorter events, 147.5 us)
Async XLA Ops:
  7.2 60.4 %all-gather.2.cloned.1.call-start = ((), (), s32[]{:S(2)}) async-start(), calls=%async_computation.1 | async-start | bytes 8650752 | tf_op jit(solution)/shard_map/all_gather | solution.py:21
  8.9 651.2 %reduce-scatter.2.cloned.1.call-start = ((), (), s32[]{:S(2)}) async-start(), calls=%async_computation.2 | async-start | bytes 17301504 | tf_op jit(solution)/shard_map/reduce_scatter | solution.py:43
  547.0 260.5 %all-reduce.4.cloned.1.call-start = ((), (), s32[]{:S(2)}) async-start(), calls=%async_computation.3 | async-start | bytes 524288 | tf_op jit(solution)/shard_map/psum | solution.py:48
Sparse Core Ops, SparseCore 0:
  10.8 56.6 all-gather.1
  547.2 112.9 reduce-scatter.1
  665.5 142.0 all-reduce.3
where the time goes:
time: 881 us; the launch traced here: 879 us
  waiting for transfers between devices  291 us (33%)
  other arithmetic  212 us (24%)
  blocking collectives  149 us (17%)
  local copies, waits for them, and re-layouts  122 us (14%)
  matrix products  90.6 us (10%)
  between operations  15.2 us (2%)
    scatter-add x8, other arithmetic, step(): total.at[tile_ids.reshape(-1)].add(contrib.reshape(-1, block_size, width))  157 us
    psum x1, blocking collectives, local(): rounded = lax.psum(partial_sketch, 'beam').astype(jnp.bfloat16)  149 us
    psum x1, waiting for transfers between devices, local(): gram = lax.psum(local_gram, ('pix', 'beam'))  143 us
    reduce_scatter x1, waiting for transfers between devices, local(): range_rows = lax.psum_scatter(total, 'pix', scatter_dimension=1, tiled=True)  113 us
    gather x8, local copies, waits for them, and re-layouts, pixel_pass(): picked = full_sketch[tile_ids]  49.9 us
    dot_general x8, matrix products, step(): jnp.einsum('tsab,tak->tsbk', tile_gains, tile_rows, preferred_element_typ...  48.8 us
    dot_general x8, matrix products, pixel_pass(): jnp.einsum('tsab,tsbk->tak', tile_gains, picked, preferred_element_type=j...  37.1 us
    all_gather x1, waiting for transfers between devices, local(): full_sketch = lax.all_gather(sketch, 'pix', axis=1, tiled=True)  35.3 us
  transfers between devices with their start and end apart: 3, of which 3 were waited for; matrix products, arithmetic and copies ran while one was open for 3% of the time, Pallas kernels for 0%

commit v1 on v0

v1 whole, which is shorter than its diff:
```python
import functools

import jax
import jax.numpy as jnp
from jax import lax
from jax.experimental import pallas as pl
from jax.experimental.pallas import tpu as pltpu
from jax.sharding import PartitionSpec as P

BEAMS = 65536
BF = jnp.bfloat16
F32 = jnp.float32
MESH = pl.DeviceIdType.MESH
MIB = 1 << 20


def place():
    pix = lax.axis_index("pix")
    y = lax.axis_index("beam")
    core = lax.rem(pix, 2)
    x = lax.rem(lax.div(pix, 2), 4)
    z = lax.div(pix, 8)
    return pix, y, z, x, core


def step4(v, d):
    return lax.rem(v + d, 4)


def neighbours():
    pix, y, z, x, core = place()

    def at(zz, xx, cc):
        return ((zz * 4 + xx) * 2 + cc, y)

    return dict(
        xr=at(z, step4(x, 1), core),
        xl=at(z, step4(x, 3), core),
        zr=at(step4(z, 1), x, core),
        zl=at(step4(z, 3), x, core),
        sib=at(z, x, 1 - core),
        yr=(pix, step4(y, 1)),
        yl=(pix, step4(y, 3)),
    )


def greet(names, near):
    barrier = pltpu.get_barrier_semaphore()
    for name in names:
        pl.semaphore_signal(barrier, inc=1, device_id=near[name], device_id_type=MESH)
    pl.semaphore_wait(barrier, len(names))


CHUNKS = 8


def pixel_kernel(
    cov, sk, gains, out, raw, om, gbuf, zf, zs, zb, got, csend,
    gsend, grecv, bsend, brecv, local,
):
    pix, y, z, x, core = place()
    near = neighbours()

    def load(i):
        return pltpu.make_async_copy(
            gains.at[pl.ds(8 * i, 8)], gbuf.at[pl.ds(8 * i, 8)], local.at[i]
        )

    mine = pltpu.make_async_copy(sk, raw.at[z, x, core], local.at[CHUNKS])
    mine.start()
    greet(("xr", "xl", "zr", "zl", "sib", "yr", "yl"), near)
    mine.wait()

    def send(k, ref, to):
        return pltpu.make_async_remote_copy(
            src_ref=ref, dst_ref=ref, send_sem=gsend.at[k], recv_sem=grecv.at[k],
            device_id=near[to], device_id_type=MESH,
        )

    lo, hi = pl.ds(0, 256), pl.ds(256, 256)
    a1 = raw.at[z, x, core, lo]
    b1 = raw.at[z, x, core, hi]
    cp = {}

    def go(k, ref, to):
        cp[k] = send(k, ref, to)
        cp[k].start()

    go(0, a1, "xr")
    go(1, a1, "xl")
    go(2, b1, "zr")
    go(3, b1, "zl")
    for i in range(CHUNKS):
        load(i).start()
    xm, xp, xo = step4(x, 3), step4(x, 1), step4(x, 2)
    zm, zp, zo = step4(z, 3), step4(z, 1), step4(z, 2)
    cp[0].wait_recv()
    go(4, raw.at[z, xm, core, pl.ds(0, 128)], "xr")
    cp[1].wait_recv()
    go(5, raw.at[z, xp, core, pl.ds(128, 128)], "xl")
    cp[2].wait_recv()
    go(6, raw.at[zm, x, core, pl.ds(256, 128)], "zr")
    cp[3].wait_recv()
    go(7, raw.at[zp, x, core, pl.ds(384, 128)], "zl")
    cp[4].wait_recv()
    cp[5].wait_recv()
    row = raw.at[z, :, core, lo]
    go(8, row, "zr")
    go(9, row, "zl")
    cp[6].wait_recv()
    cp[7].wait_recv()
    col = raw.at[:, x, core, hi]
    go(10, col, "xr")
    go(11, col, "xl")
    go(12, row, "sib")
    go(13, col, "sib")
    cp[8].wait_recv()
    go(14, raw.at[zm, pl.ds(0, 2), core, lo], "zr")
    cp[9].wait_recv()
    go(15, raw.at[zp, pl.ds(2, 2), core, lo], "zl")
    cp[10].wait_recv()
    go(16, raw.at[pl.ds(0, 2), xm, core, hi], "xr")
    cp[11].wait_recv()
    go(17, raw.at[pl.ds(2, 2), xp, core, hi], "xl")
    go(18, raw.at[zm, :, core, lo], "sib")
    go(19, raw.at[zp, :, core, lo], "sib")
    go(20, raw.at[:, xm, core, hi], "sib")
    go(21, raw.at[:, xp, core, hi], "sib")
    cp[14].wait_recv()
    cp[15].wait_recv()
    go(22, raw.at[zo, :, core, lo], "sib")
    cp[16].wait_recv()
    cp[17].wait_recv()
    go(23, raw.at[:, xo, core, hi], "sib")
    for k in (12, 13, 18, 19, 20, 21, 22, 23):
        cp[k].wait_recv()

    o = lax.broadcasted_iota(jnp.int32, (256, 256), 0)
    c = lax.broadcasted_iota(jnp.int32, (256, 256), 1)
    from_row = ((o % 64) // 4) * 16 + (o // 64) * 4 + o % 4
    swap = (c == from_row).astype(F32).astype(BF)

    @pl.loop(0, 32)
    def _(q):
        for g in range(2):
            part = raw[pl.ds(2 * g, 2), :, :, pl.ds(pl.multiple_of(16 * q, 16), 16), :]
            part = part.reshape(256, 256)
            turned = jnp.dot(swap, part, preferred_element_type=F32).astype(BF)
            om[pl.ds(4 * q, 4), pl.ds(64 * g, 64), :] = turned.reshape(4, 64, 256)

    c0, c1, c2, c3 = y, step4(y, 1), step4(y, 2), step4(y, 3)

    def rc(k, i, src, dst, to):
        return pltpu.make_async_remote_copy(
            src_ref=src, dst_ref=dst, send_sem=bsend.at[k, i], recv_sem=brecv.at[k, i],
            device_id=near[to], device_id_type=MESH,
        )

    def copies(i):
        t = 8 * i
        own = zb.at[pl.ds(t + 2 * c0, 2)]
        left = zb.at[t + 2 * c3]
        right = zb.at[t + 2 * c1 + 1]
        table = (
            (zs.at[t + 2 * c2], got.at[0, i], "yr"),
            (zs.at[t + 2 * c1 + 1], got.at[1, i], "yr"),
            (zs.at[t + 2 * c2 + 1], got.at[2, i], "yl"),
            (zs.at[t + 2 * c3], got.at[3, i], "yl"),
            (csend.at[0, i], got.at[4, i], "yr"),
            (csend.at[1, i], got.at[5, i], "yl"),
            (own, own, "yr"),
            (own, own, "yl"),
            (left, left, "yr"),
            (right, right, "yl"),
        )
        return lambda k: rc(k, i, *table[k])

    def store(i):
        return pltpu.make_async_copy(
            zb.at[pl.ds(8 * i, 8)], out.at[pl.ds(8 * i, 8)], local.at[CHUNKS + 1 + i]
        )

    @pl.loop(0, CHUNKS + 4)
    def _(tau):
        @pl.when(tau < CHUNKS)
        def _():
            load(tau).wait()

            @pl.loop(0, 8)
            def _(tt):
                t = tau * 8 + tt
                lhs = jnp.concatenate([gbuf[t, s] for s in range(8)], axis=1)
                rhs = jnp.concatenate([om[cov[t * 8 + s]] for s in range(8)], axis=0)
                acc = jnp.dot(lhs, rhs, preferred_element_type=F32)
                zf[t] = acc
                zs[t] = acc.astype(BF)

            m = copies(tau)
            for k in range(4):
                m(k).start()

        @pl.when(jnp.logical_and(tau >= 1, tau < CHUNKS + 1))
        def _():
            i = tau - 1
            m = copies(i)
            m(0).wait_recv()
            csend[0, i] = (got[0, i].astype(F32) + zf[8 * i + 2 * c1]).astype(BF)
            m(4).start()
            m(2).wait_recv()
            csend[1, i] = (got[2, i].astype(F32) + zf[8 * i + 2 * c3 + 1]).astype(BF)
            m(5).start()

        @pl.when(jnp.logical_and(tau >= 2, tau < CHUNKS + 2))
        def _():
            i = tau - 2
            m = copies(i)
            m(3).wait_recv()
            m(4).wait_recv()
            t = 8 * i + 2 * c0
            zb[t] = (zf[t] + got[3, i].astype(F32) + got[4, i].astype(F32)).astype(BF)
            m(1).wait_recv()
            m(5).wait_recv()
            zb[t + 1] = (zf[t + 1] + got[1, i].astype(F32) + got[5, i].astype(F32)).astype(BF)
            m(6).start()
            m(7).start()

        @pl.when(jnp.logical_and(tau >= 3, tau < CHUNKS + 3))
        def _():
            m = copies(tau - 3)
            m(6).wait_recv()
            m(8).start()
            m(7).wait_recv()
            m(9).start()

        @pl.when(tau >= 4)
        def _():
            m = copies(tau - 4)
            m(8).wait_recv()
            m(9).wait_recv()
            store(tau - 4).start()

    for k in range(24):
        cp[k].wait_send()

    @pl.loop(0, CHUNKS)
    def _(i):
        m = copies(i)
        for k in range(10):
            m(k).wait_send()
        store(i).wait()


def pixel_pass(sketch, gains, coverage):
    scratch = [
        pltpu.VMEM((4, 4, 2, 512, 256), BF),
        pltpu.VMEM((128, 128, 256), BF),
        pltpu.VMEM((64, 8, 128, 128), BF),
        pltpu.VMEM((64, 128, 256), F32),
        pltpu.VMEM((64, 128, 256), BF),
        pltpu.VMEM((64, 128, 256), BF),
        pltpu.VMEM((6, CHUNKS, 128, 256), BF),
        pltpu.VMEM((2, CHUNKS, 128, 256), BF),
        pltpu.SemaphoreType.DMA((24,)),
        pltpu.SemaphoreType.DMA((24,)),
        pltpu.SemaphoreType.DMA((10, CHUNKS)),
        pltpu.SemaphoreType.DMA((10, CHUNKS)),
        pltpu.SemaphoreType.DMA((2 * CHUNKS + 1,)),
    ]
    return pl.pallas_call(
        pixel_kernel,
        out_shape=jax.ShapeDtypeStruct((64, 128, 256), BF),
        in_specs=[
            pl.BlockSpec(memory_space=pltpu.SMEM),
            pl.BlockSpec(memory_space=pl.ANY),
            pl.BlockSpec(memory_space=pl.ANY),
        ],
        out_specs=pl.BlockSpec(memory_space=pl.ANY),
        scratch_shapes=scratch,
        compiler_params=pltpu.CompilerParams(
            collective_id=0, has_side_effects=True, vmem_limit_bytes=60 * MIB
        ),
        cost_estimate=pl.CostEstimate(
            flops=6_500_000_000, bytes_accessed=22_000_000, transcendentals=0
        ),
        name="pixel_pass",
    )(coverage.reshape(-1), sketch.reshape(512, 256), gains)


TILES_STEP = 4


def beam_kernel(cov, g, zb, out, acc, split, sems):
    step = pl.program_id(0)

    @pl.when(step == 0)
    def _():
        @pl.loop(0, 128)
        def _(b):
            acc[b] = jnp.zeros((128, 256), F32)

    for tt in range(TILES_STEP):
        rows = zb[tt]
        for s in range(8):
            b = cov[(step * TILES_STEP + tt) * 8 + s]
            acc[b] += lax.dot_general(
                g[tt, s], rows, (((0,), (0,)), ((), ())), preferred_element_type=F32
            )

    @pl.when(step == pl.num_programs(0) - 1)
    def _():
        low = lax.broadcasted_iota(jnp.int32, (16, 8, 256), 1) < 4

        def store(i):
            return pltpu.make_async_copy(
                split.at[:, :, pl.ds(pl.multiple_of(64 * i, 64), 64)],
                out.at[:, :, pl.ds(pl.multiple_of(64 * i, 64), 64)],
                sems.at[i],
            )

        @pl.loop(0, 8)
        def _(i):
            @pl.loop(0, 8)
            def _(j):
                pair = i * 8 + j
                a = acc[2 * pair].reshape(16, 8, 256)
                b = acc[2 * pair + 1].reshape(16, 8, 256)
                at = pl.ds(pl.multiple_of(8 * pair, 8), 8)
                split[:, 0, at, :] = jnp.where(low, a, pltpu.roll(b, 4, 1))
                split[:, 1, at, :] = jnp.where(low, pltpu.roll(a, 4, 1), b)

            store(i).start()

        @pl.loop(0, 8)
        def _(i):
            store(i).wait()


def beam_pass(coverage, gains, rounded):
    spec = pltpu.PrefetchScalarGridSpec(
        num_scalar_prefetch=1,
        grid=(64 // TILES_STEP,),
        in_specs=[
            pl.BlockSpec((TILES_STEP, 8, 128, 128), lambda i, c: (i, 0, 0, 0)),
            pl.BlockSpec((TILES_STEP, 128, 256), lambda i, c: (i, 0, 0)),
        ],
        out_specs=pl.BlockSpec(memory_space=pl.ANY),
        scratch_shapes=[
            pltpu.VMEM((128, 128, 256), F32),
            pltpu.VMEM((16, 2, 512, 256), F32),
            pltpu.SemaphoreType.DMA((8,)),
        ],
    )
    return pl.pallas_call(
        beam_kernel,
        grid_spec=spec,
        out_shape=jax.ShapeDtypeStruct((16, 2, 512, 256), F32),
        compiler_params=pltpu.CompilerParams(vmem_limit_bytes=56 * MIB),
        cost_estimate=pl.CostEstimate(
            flops=4_300_000_000, bytes_accessed=38_000_000, transcendentals=0
        ),
        name="beam_pass",
    )(coverage.reshape(-1), gains, rounded)


def local(sketch, gains, coverage):
    rounded = pixel_pass(sketch, gains, coverage)
    total = beam_pass(coverage, gains, rounded)
    flat = lax.psum_scatter(
        total.reshape(32, 512, 256), "pix", scatter_dimension=0, tiled=False
    )
    local_gram = jnp.dot(
        flat.T, flat, precision=lax.Precision.HIGHEST, preferred_element_type=F32
    )
    gram = lax.psum(local_gram, ("pix", "beam"))
    lower = jnp.linalg.cholesky(gram)
    solved = jax.scipy.linalg.solve_triangular(lower, flat.T, lower=True).T
    scale = jnp.sqrt(jnp.float32(BEAMS))
    return ((solved * scale).reshape(sketch.shape), lower.T / scale)


def solution(mesh):
    return jax.shard_map(
        local,
        mesh=mesh,
        in_specs=(P("beam", "pix", None), P("pix", "beam", None, None), P("pix", "beam")),
        out_specs=(P("beam", "pix", None), P()),
        check_vma=False,
    )
```

time: 881 us -> 490 us (0.56)
  other arithmetic: 212 us -> 54.8 us
  blocking collectives: 149 us -> 0 us
  Pallas kernels: 0 us -> 144 us
  local copies, waits for them, and re-layouts: 122 us -> 10.4 us
  matrix products: 90.6 us -> 6.7 us
  waiting for transfers between devices: 291 us -> 257 us
    scatter-add x8 -> x0, other arithmetic: 157 us -> none  [step(): total.at[tile_ids.reshape(-1)].add(contrib.reshape(-1, block_size, width))]
    psum x1 -> x0, blocking collectives: 149 us -> none  [local(): rounded = lax.psum(partial_sketch, 'beam').astype(jnp.bfloat16)]
    pallas_call x0 -> x2, Pallas kernels: none -> 144 us  [the longest x1 119 us: pixel_pass(): pl.pallas_call(pixel_kernel, out_shape=jax.ShapeDtypeStruct((64, 128, 256...]
    dot_general x16 -> x0, matrix products: 86 us -> none  [the longest x8 48.8 us: step(): jnp.einsum('tsab,tak->tsbk', tile_gains, tile_rows, preferred_element_typ...]
    gather x8 -> x0, local copies, waits for them, and re-layouts: 49.9 us -> none  [pixel_pass(): picked = full_sketch[tile_ids]]
    all_gather x1 -> x0, waiting for transfers between devices: 35.3 us -> none  [local(): full_sketch = lax.all_gather(sketch, 'pix', axis=1, tiled=True)]
    while x2 -> x0, local copies, waits for them, and re-layouts: 29.1 us -> none  [the longest x1 17.7 us: local(): total, _ = lax.scan(step, empty, (grouped_gains, grouped_ids, grouped_rows))]
    unnamed x4 -> x2, local copies, waits for them, and re-layouts: 25.7 us -> 1.61 us
  transfers between devices with their start and end apart: 3 -> 2, of which waited for: 3 -> 2; matrix products, arithmetic and copies ran while one was open for 3% -> 0% of each run, Pallas kernels for 0% -> 0%
where the time goes in v1:
time: 490 us; the launch traced here: 489 us
  waiting for transfers between devices  257 us (52%)
  Pallas kernels  144 us (29%)
  other arithmetic  54.8 us (11%)
  between operations  15.5 us (3%)
  local copies, waits for them, and re-layouts  10.4 us (2%)
  matrix products  6.7 us (1%)
    psum x1, waiting for transfers between devices, local(): gram = lax.psum(local_gram, ('pix', 'beam'))  144 us
    pallas_call x1, Pallas kernels, pixel_pass(): pl.pallas_call(pixel_kernel, out_shape=jax.ShapeDtypeStruct((64, 128, 256...  119 us
    reduce_scatter x1, waiting for transfers between devices, local(): lax.psum_scatter(total.reshape(32, 512, 256), 'pix', scatter_dimension=0,...  112 us
    another operation x6, other arithmetic, local(): lower = jnp.linalg.cholesky(gram)  34 us
    pallas_call x1, Pallas kernels, beam_pass(): pl.pallas_call(beam_kernel, grid_spec=spec, out_shape=jax.ShapeDtypeStruc...  25.4 us
    another operation x2, other arithmetic, local(): solved = jax.scipy.linalg.solve_triangular(lower, flat.T, lower=True).T  19.7 us
  transfers between devices with their start and end apart: 2, of which 2 were waited for; matrix products, arithmetic and copies ran while one was open for 0% of the time, Pallas kernels for 0%

profile of v1, /device:TPU:1, one launch (start us, length us, event | category | flops | bytes accessed | tf_op | source)
XLA Modules:
  0.0 488.8 jit_solution(5776049826526962967)
XLA Ops:
  7.2 0.8 copy.9
  8.0 0.7 reshape.36.cov
  8.7 1.7 reshape.37.sk
  10.4 118.5 %pixel_pass.1.zb = bf16[64,128,256]{2,1,0:T(8,128)(2,1)} custom-call(s32[512]{0:T(512)} %reshape.36.cov, bf16[512,256]{1,0:T(8,128)(2,1)} %reshape.37.sk, bf16[64,8,128,128]{3,2,1,0:T(8,128)(2,1)} %g.1), custom_call_target="tpu_custom_call" | custom-call | flops 6499999744 | bytes 22000000 | tf_op jit(solution)/shard_map/pixel_pass/pallas_call | solution.py:269
  128.9 25.4 %beam_pass.1 = f32[16,2,512,256]{3,2,1,0:T(8,128)} custom-call(s32[512]{0:T(512)} %reshape.36.cov, bf16[64,8,128,128]{3,2,1,0:T(8,128)(2,1)} %g.1, bf16[64,128,256]{2,1,0:T(8,128)(2,1)} %pixel_pass.1.zb), custom_call_target="tpu_custom_call" | custom-call | flops 4300000256 | bytes 38000000 | tf_op jit(solution)/shard_map/beam_pass/pallas_call | solution.py:353
  154.6 112.5 %reduce-scatter.2.cloned.1.call-done = f32[1,512,256]{2,1,0:T(8,128)} async-done(((f32[32,512,256]{2,1,0:T(8,128)}), f32[1,512,256]{2,1,0:T(8,128)}) %reduce-scatter.2.cloned.1.call-update) | async-done | bytes 524304 | tf_op jit(solution)/shard_map/reduce_scatter | solution.py:368
  267.1 2.9 fusion.1
  270.0 144.5 %all-reduce.3.cloned.1.call-done = f32[256,256]{0,1:T(8,128)} async-done(((f32[256,256]{0,1:T(8,128)}), f32[256,256]{0,1:T(8,128)}) %all-reduce.3.cloned.1.call-update) | async-done | bytes 262160 | tf_op jit(solution)/shard_map/psum | solution.py:374
  414.5 1.1 copy.11
  415.6 1.0 fusion.5
  416.6 11.7 %cholesky.50 = f32[128,128]{1,0:T(8,128)S(1)} custom-call(f32[128,128]{1,0:T(8,128)S(1)} %cholesky.118), custom_call_target="Cholesky" | custom-call | tf_op jit(solution)/shard_map/jit(cholesky)/cholesky | solution.py:375
  428.4 9.8 %custom-call.15 = f32[1,128,128]{1,2,0:T(8,128)S(1)} custom-call(f32[1,128,128]{2,1,0:T(8,128)S(1)} %get-tuple-element.29), custom_call_target="InvertDiagBlocksLowerTriangular" | custom-call | tf_op jit(solution)/shard_map/jit(cholesky)/cholesky | solution.py:375
  438.7 11.7 %cholesky.105 = f32[128,128]{1,0:T(8,128)S(1)} custom-call(f32[128,128]{1,0:T(8,128)S(1)} %convolution_subtract_fusion.1), custom_call_target="Cholesky" | custom-call | tf_op jit(solution)/shard_map/jit(cholesky)/cholesky | solution.py:375
  450.4 0.7 compare_reduce_fusion
  452.6 4.3 while.1
  452.8 0.6 fusion.18
  453.4 1.4 bitcast_dynamic-update-slice_fusion.2
  454.9 0.6 fusion.18
  455.5 1.4 bitcast_dynamic-update-slice_fusion.2
  456.9 19.7 %custom-call.16 = f32[2,128,128]{1,2,0:T(8,128)S(1)} custom-call(f32[2,128,128]{2,1,0:T(8,128)S(1)} %get-tuple-element.9), custom_call_target="InvertDiagBlocksLowerTriangular" | custom-call | tf_op jit(solution)/shard_map/jit(_solve_triangular)/triangular_solve | solution.py:376
  476.6 1.4 fusion.3
  478.0 1.5 convolution_subtract_fusion
  480.2 0.9 reshape.39
  481.1 0.8 copy.13
  (19 shorter events, 1.6 us)
Async XLA Ops:
  7.2 259.9 %reduce-scatter.2.cloned.1.call-start = ((), (), s32[]{:S(2)}) async-start(), calls=%async_computation.1 | async-start | bytes 17301504 | tf_op jit(solution)/shard_map/reduce_scatter | solution.py:368
  154.4 260.1 %all-reduce.3.cloned.1.call-start = ((), (), s32[]{:S(2)}) async-start(), calls=%async_computation.2 | async-start | bytes 524288 | tf_op jit(solution)/shard_map/psum | solution.py:374
Sparse Core Ops, SparseCore 0:
  154.5 112.5 reduce-scatter.1
  272.4 142.0 all-reduce.2

commit v2 on v1

--- a/solution.py
+++ b/solution.py
@@ -41,6 +41,9 @@
         sib=at(z, x, 1 - core),
         yr=(pix, step4(y, 1)),
         yl=(pix, step4(y, 3)),
+        xo=at(z, step4(x, 2), core),
+        zo=at(step4(z, 2), x, core),
+        yo=(pix, step4(y, 2)),
     )
 
 
@@ -361,17 +364,239 @@
         name="beam_pass",
     )(coverage.reshape(-1), gains, rounded)
 
+SUB = 4
+ROWS = 256 // SUB
+HALF = ROWS // 2
+
+
+def sum_kernel(
+    part, flat, gram, own, sib, got1, got2, gacc, gout, gsib, gx, gz, gy,
+    csend, crecv, rsend, rrecv, gsend, grecv, local,
+):
+    pix, y, z, x, core = place()
+    near = neighbours()
+    other = 1 - core
+
+    def rows(h, j):
+        return pl.ds(pl.multiple_of(256 * h + ROWS * j, ROWS), ROWS)
+
+    def load(h, j):
+        return pltpu.make_async_copy(
+            part.at[:, :, core, rows(h, j)], own.at[h, j], local.at[h, j]
+        )
+
+    def swap(h, j):
+        return pltpu.make_async_remote_copy(
+            src_ref=part.at[:, :, other, rows(h, j)], dst_ref=sib.at[h, j],
+            send_sem=csend.at[h, j], recv_sem=crecv.at[h, j],
+            device_id=near["sib"], device_id_type=MESH,
+        )
+
+    for j in range(SUB):
+        for h in range(2):
+            load(h, j).start()
+    greet(("xr", "xl", "zr", "zl", "sib", "yr", "yl", "xo", "zo", "yo"), near)
+    for j in range(SUB):
+        for h in range(2):
+            swap(h, j).start()
+
+    def ring(h, phase):
+        if (h == 0) == (phase == 0):
+            return x, "xr", "xl"
+        return z, "zr", "zl"
+
+    def piece(h, j, phase, d, lo):
+        if phase == 0:
+            two = pl.ds(0 if lo else 2, 2)
+            return own.at[h, j, two, d] if h == 0 else own.at[h, j, d, two]
+        n = pl.ds(0 if lo else HALF, HALF)
+        return own.at[h, j, d, x, n] if h == 0 else own.at[h, j, z, d, n]
+
+    def msg(h, j, phase, k):
+        c, right, left = ring(h, phase)
+        got = got1 if phase == 0 else got2
+        d, lo, to = (
+            (step4(c, 2), True, right),
+            (step4(c, 1), False, right),
+            (step4(c, 2), False, left),
+            (step4(c, 3), True, left),
+            (step4(c, 1), True, right),
+            (step4(c, 3), False, left),
+        )[k]
+        return pltpu.make_async_remote_copy(
+            src_ref=piece(h, j, phase, d, lo), dst_ref=got.at[h, j, k],
+            send_sem=rsend.at[h, j, phase, k], recv_sem=rrecv.at[h, j, phase, k],
+            device_id=near[to], device_id_type=MESH,
+        )
+
+    def first(h, j, phase):
+        for k in range(4):
+            msg(h, j, phase, k).start()
+
+    def second(h, j, phase):
+        c = ring(h, phase)[0]
+        got = got1 if phase == 0 else got2
+        msg(h, j, phase, 0).wait_recv()
+        mid = piece(h, j, phase, step4(c, 1), True)
+        mid[...] += got[h, j, 0]
+        msg(h, j, phase, 4).start()
+        msg(h, j, phase, 2).wait_recv()
+        mid = piece(h, j, phase, step4(c, 3), False)
+        mid[...] += got[h, j, 2]
+        msg(h, j, phase, 5).start()
+
+    def finish(h, j, phase):
+        c = ring(h, phase)[0]
+        got = got1 if phase == 0 else got2
+        for k in (3, 4, 1, 5):
+            msg(h, j, phase, k).wait_recv()
+        lo = piece(h, j, phase, c, True)
+        lo[...] += got[h, j, 3] + got[h, j, 4]
+        hi = piece(h, j, phase, c, False)
+        hi[...] += got[h, j, 1] + got[h, j, 5]
+
+    def stage(tau, after, work):
+        @pl.when(jnp.logical_and(tau >= after, tau < after + SUB))
+        def _():
+            for h in range(2):
+                work(h, tau - after)
+
+    @pl.loop(0, SUB + 4)
+    def _(tau):
+        def begin(h, j):
+            load(h, j).wait()
+            swap(h, j).wait_recv()
+
+            @pl.loop(0, 4)
+            def _(i):
+                own[h, j, i] += sib[h, j, i]
+
+            first(h, j, 0)
+
+        def turn(h, j):
+            finish(h, j, 0)
+            first(h, j, 1)
+
+        def end(h, j):
+            finish(h, j, 1)
+            flat[rows(h, j), :] = own[h, j, z, x]
+
+        stage(tau, 0, begin)
+        stage(tau, 1, lambda h, j: second(h, j, 0))
+        stage(tau, 2, turn)
+        stage(tau, 3, lambda h, j: second(h, j, 1))
+        stage(tau, 4, end)
+
+    f = flat[...]
+    gacc[...] = lax.dot_general(
+        f, f, (((0,), (0,)), ((), ())),
+        precision=lax.Precision.HIGHEST, preferred_element_type=F32,
+    )
+
+    def gmsg(k, src, dst, to):
+        return pltpu.make_async_remote_copy(
+            src_ref=src, dst_ref=dst, send_sem=gsend.at[k], recv_sem=grecv.at[k],
+            device_id=near[to], device_id_type=MESH,
+        )
+
+    def block(at, n, ref=gacc):
+        return ref.at[pl.ds(pl.multiple_of(at, n), n)]
+
+    sent = []
+
+    def exchange(k, pairs):
+        todo = [gmsg(k + n, *p) for n, p in enumerate(pairs)]
+        for m in todo:
+            m.start()
+        for m in todo:
+            m.wait_recv()
+        sent.extend(todo)
+
+    base = 128 * core
+    exchange(0, [(block(128 * other, 128), gsib, "sib")])
+    mine = block(base, 128)
+    mine[...] += gsib[...]
+    xat = base + 32 * x
+    exchange(1, [
+        (block(base + 32 * step4(x, d), 32), gx.at[d - 1], to)
+        for d, to in ((1, "xr"), (2, "xo"), (3, "xl"))
+    ])
+    mine = block(xat, 32)
+    mine[...] += gx[0] + gx[1] + gx[2]
+    zat = xat + 8 * z
+    exchange(4, [
+        (block(xat + 8 * step4(z, d), 8), gz.at[d - 1], to)
+        for d, to in ((1, "zr"), (2, "zo"), (3, "zl"))
+    ])
+    mine = block(zat, 8)
+    gy[y] = mine[...] + (gz[0] + gz[1] + gz[2])
+    exchange(7, [(gy.at[y], gy.at[y], to) for to in ("yr", "yo", "yl")])
+    mine = block(zat, 8, gout)
+    mine[...] = (gy[0] + gy[1]) + (gy[2] + gy[3])
+    exchange(10, [(mine, mine, to) for to in ("zr", "zo", "zl")])
+    mine = block(xat, 32, gout)
+    exchange(13, [(mine, mine, to) for to in ("xr", "xo", "xl")])
+    mine = block(base, 128, gout)
+    exchange(16, [(mine, mine, "sib")])
+    gram[...] = gout[...]
+    for m in sent:
+        m.wait_send()
+
+    @pl.loop(0, SUB)
+    def _(j):
+        for h in range(2):
+            swap(h, j).wait_send()
+            for phase in range(2):
+                for k in range(6):
+                    msg(h, j, phase, k).wait_send()
+
+
+def sum_pass(total):
+    scratch = [
+        pltpu.VMEM((2, SUB, 4, 4, ROWS, 256), F32),
+        pltpu.VMEM((2, SUB, 4, 4, ROWS, 256), F32),
+        pltpu.VMEM((2, SUB, 6, 2, ROWS, 256), F32),
+        pltpu.VMEM((2, SUB, 6, HALF, 256), F32),
+        pltpu.VMEM((256, 256), F32),
+        pltpu.VMEM((256, 256), F32),
+        pltpu.VMEM((128, 256), F32),
+        pltpu.VMEM((3, 32, 256), F32),
+        pltpu.VMEM((3, 8, 256), F32),
+        pltpu.VMEM((4, 8, 256), F32),
+        pltpu.SemaphoreType.DMA((2, SUB)),
+        pltpu.SemaphoreType.DMA((2, SUB)),
+        pltpu.SemaphoreType.DMA((2, SUB, 2, 6)),
+        pltpu.SemaphoreType.DMA((2, SUB, 2, 6)),
+        pltpu.SemaphoreType.DMA((17,)),
+        pltpu.SemaphoreType.DMA((17,)),
+        pltpu.SemaphoreType.DMA((2, SUB)),
+    ]
+    return pl.pallas_call(
+        sum_kernel,
+        out_shape=(
+            jax.ShapeDtypeStruct((512, 256), F32),
+            jax.ShapeDtypeStruct((256, 256), F32),
+        ),
+        in_specs=[pl.BlockSpec(memory_space=pl.ANY)],
+        out_specs=(
+            pl.BlockSpec(memory_space=pltpu.VMEM),
+            pl.BlockSpec(memory_space=pltpu.VMEM),
+        ),
+        scratch_shapes=scratch,
+        compiler_params=pltpu.CompilerParams(
+            collective_id=1, has_side_effects=True, vmem_limit_bytes=48 * MIB
+        ),
+        cost_estimate=pl.CostEstimate(
+            flops=500_000_000, bytes_accessed=18_000_000, transcendentals=0
+        ),
+        name="sum_pass",
+    )(total)
+
 
 def local(sketch, gains, coverage):
     rounded = pixel_pass(sketch, gains, coverage)
     total = beam_pass(coverage, gains, rounded)
-    flat = lax.psum_scatter(
-        total.reshape(32, 512, 256), "pix", scatter_dimension=0, tiled=False
-    )
-    local_gram = jnp.dot(
-        flat.T, flat, precision=lax.Precision.HIGHEST, preferred_element_type=F32
-    )
-    gram = lax.psum(local_gram, ("pix", "beam"))
+    flat, gram = sum_pass(total.reshape(4, 4, 2, 512, 256))
     lower = jnp.linalg.cholesky(gram)
     solved = jax.scipy.linalg.solve_triangular(lower, flat.T, lower=True).T
     scale = jnp.sqrt(jnp.float32(BEAMS))

time: 490 us -> 290 us (0.59)
  waiting for transfers between devices: 257 us -> 0 us
  Pallas kernels: 144 us -> 222 us
  between operations: 15.5 us -> 2.08 us
    psum x1 -> x0, waiting for transfers between devices: 144 us -> none  [local(): gram = lax.psum(local_gram, ('pix', 'beam'))]
    reduce_scatter x1 -> x0, waiting for transfers between devices: 112 us -> none  [local(): lax.psum_scatter(total.reshape(32, 512, 256), 'pix', scatter_dimension=0,...]
    pallas_call x0 -> x1, Pallas kernels: none -> 78.1 us  [sum_pass(): pl.pallas_call(sum_kernel, out_shape=(jax.ShapeDtypeStruct((512, 256), F3...]
  transfers between devices with their start and end apart: 2 -> 0, of which waited for: 2 -> 0; matrix products, arithmetic and copies ran while one was open for 0% -> 0% of each run, Pallas kernels for 0% -> 0%
where the time goes in v2:
time: 290 us; the launch traced here: 289 us
  Pallas kernels  222 us (77%)
  other arithmetic  54 us (19%)
  local copies, waits for them, and re-layouts  9.41 us (3%)
    pallas_call x1, Pallas kernels, pixel_pass(): pl.pallas_call(pixel_kernel, out_shape=jax.ShapeDtypeStruct((64, 128, 256...  119 us
    pallas_call x1, Pallas kernels, sum_pass(): pl.pallas_call(sum_kernel, out_shape=(jax.ShapeDtypeStruct((512, 256), F3...  78.1 us
    another operation x6, other arithmetic, local(): lower = jnp.linalg.cholesky(gram)  34 us
    pallas_call x1, Pallas kernels, beam_pass(): pl.pallas_call(beam_kernel, grid_spec=spec, out_shape=jax.ShapeDtypeStruc...  25.4 us
    another operation x2, other arithmetic, local(): solved = jax.scipy.linalg.solve_triangular(lower, flat.T, lower=True).T  19.9 us

profile of v2, /device:TPU:1, one launch (start us, length us, event | category | flops | bytes accessed | tf_op | source)
XLA Modules:
  0.0 289.4 jit_solution(7256629956964829244)
XLA Ops:
  0.6 0.8 copy.8
  1.4 0.7 reshape.36.cov
  2.1 1.7 reshape.37.sk
  3.8 118.5 %pixel_pass.1.zb = bf16[64,128,256]{2,1,0:T(8,128)(2,1)} custom-call(s32[512]{0:T(512)} %reshape.36.cov, bf16[512,256]{1,0:T(8,128)(2,1)} %reshape.37.sk, bf16[64,8,128,128]{3,2,1,0:T(8,128)(2,1)} %g.1), custom_call_target="tpu_custom_call" | custom-call | flops 6499999744 | bytes 22000000 | tf_op jit(solution)/shard_map/pixel_pass/pallas_call | solution.py:272
  122.3 25.4 %beam_pass.1 = f32[16,2,512,256]{3,2,1,0:T(8,128)} custom-call(s32[512]{0:T(512)} %reshape.36.cov, bf16[64,8,128,128]{3,2,1,0:T(8,128)(2,1)} %g.1, bf16[64,128,256]{2,1,0:T(8,128)(2,1)} %pixel_pass.1.zb), custom_call_target="tpu_custom_call" | custom-call | flops 4300000256 | bytes 38000000 | tf_op jit(solution)/shard_map/beam_pass/pallas_call | solution.py:356
  147.8 78.1 %sum_pass.1 = (f32[512,256]{1,0:T(8,128)S(1)}, f32[256,256]{1,0:T(8,128)S(1)}) custom-call(f32[4,4,2,512,256]{4,3,2,1,0:T(8,128)} %bitcast.39), custom_call_target="tpu_custom_call" | custom-call | flops 500000000 | bytes 18000000 | tf_op jit(solution)/shard_map/sum_pass/pallas_call | solution.py:574
  226.1 11.7 %cholesky.50 = f32[128,128]{1,0:T(8,128)S(1)} custom-call(f32[128,128]{1,0:T(8,128)S(1)} %cholesky.118), custom_call_target="Cholesky" | custom-call | tf_op jit(solution)/shard_map/jit(cholesky)/cholesky | solution.py:600
  237.8 9.8 %custom-call.15 = f32[1,128,128]{1,2,0:T(8,128)S(1)} custom-call(f32[1,128,128]{2,1,0:T(8,128)S(1)} %get-tuple-element.33), custom_call_target="InvertDiagBlocksLowerTriangular" | custom-call | tf_op jit(solution)/shard_map/jit(cholesky)/cholesky | solution.py:600
  247.6 0.2 constant_dynamic-update-slice_fusion.1
  247.9 0.3 convolution_subtract_fusion.1
  248.1 11.7 %cholesky.105 = f32[128,128]{1,0:T(8,128)S(1)} custom-call(f32[128,128]{1,0:T(8,128)S(1)} %convolution_subtract_fusion.1), custom_call_target="Cholesky" | custom-call | tf_op jit(solution)/shard_map/jit(cholesky)/cholesky | solution.py:600
  259.9 0.6 compare_reduce_fusion
  262.0 4.1 %while.1 = (s32[]{:T(128)}, f32[256,256]{1,0:T(8,128)S(1)}, s32[2,2]{1,0:T(2,128)S(1)}, f32[2,128,128]{2,1,0:T(8,128)S(1)}, s32[]{:T(128)}) while((s32[]{:T(128)}, f32[256,256]{1,0:T(8,128)S(1)}, s32[2,2]{1,0:T(2,128)S(1)}, f32[2,128,128]{2,1,0:T(8,128)S(1)}, s32[]{:T(128)}) %tuple.30), condition=%wide.while_cond, body=%wide.while_body.sunk | while | flops 2 | bytes 131181 | solution.py:601
  262.0 0.6 fusion.16
  262.6 1.4 bitcast_dynamic-update-slice_fusion.2
  264.0 0.6 fusion.16
  264.6 1.4 bitcast_dynamic-update-slice_fusion.2
  266.1 19.9 %custom-call.16 = f32[2,128,128]{1,2,0:T(8,128)S(1)} custom-call(f32[2,128,128]{2,1,0:T(8,128)S(1)} %get-tuple-element.13), custom_call_target="InvertDiagBlocksLowerTriangular" | custom-call | tf_op jit(solution)/shard_map/jit(_solve_triangular)/triangular_solve | solution.py:601
  286.0 0.4 fusion.1
  286.4 0.6 convolution_subtract_fusion
  287.0 0.4 fusion.6
  287.5 0.2 copy.10
  287.7 0.9 reshape.39
  288.6 0.8 copy.11
  (13 shorter events, 0.4 us)

commit v3 on v2

--- a/solution.py
+++ b/solution.py
@@ -592,15 +592,95 @@
         name="sum_pass",
     )(total)
 
+PIVOTS = 4
+
+
+def eliminate(a):
+    sub = lax.broadcasted_iota(jnp.int32, (8, 128), 0)
+    lane = lax.broadcasted_iota(jnp.int32, (8, 128), 1)
+    rows = [a[8 * i : 8 * i + 8] for i in range(16)]
+    inv = [(lane == sub + 8 * i).astype(F32) for i in range(16)]
+    for start in range(0, 128, PIVOTS):
+        g = start // 8
+        cols = [
+            [jnp.broadcast_to(r[:, j : j + 1], (8, 128)) for r in rows[g:]]
+            for j in range(start, start + PIVOTS)
+        ]
+        for k in range(PIVOTS):
+            at = start + k - 8 * g
+            one = jnp.broadcast_to(cols[k][0][at : at + 1], (8, 128))
+            scale = 1.0 / one
+            head = jnp.broadcast_to(rows[g][at : at + 1], (8, 128))
+            head_inv = jnp.broadcast_to(inv[g][at : at + 1], (8, 128))
+            heads = [
+                jnp.broadcast_to(cols[m][0][at : at + 1], (8, 128))
+                for m in range(k + 1, PIVOTS)
+            ]
+            for i in range(g, 16):
+                f = cols[k][i - g] * scale
+                if i == g:
+                    f = jnp.where(sub > at, f, 0.0)
+                for n, m in enumerate(range(k + 1, PIVOTS)):
+                    cols[m][i - g] = cols[m][i - g] - f * heads[n]
+                rows[i] = rows[i] - f * head
+                inv[i] = inv[i] - f * head_inv
+    u = jnp.concatenate(rows, axis=0)
+    w = jnp.concatenate(inv, axis=0)
+    return u, w
+
+
+def mm(a, b, ca=1, cb=0):
+    return lax.dot_general(
+        a, b, (((ca,), (cb,)), ((), ())),
+        precision=lax.Precision.HIGHEST, preferred_element_type=F32,
+    )
+
+
+def factor_half(a):
+    u, w = eliminate(a)
+    r = lax.broadcasted_iota(jnp.int32, (128, 128), 0)
+    c = lax.broadcasted_iota(jnp.int32, (128, 128), 1)
+    d = jnp.sum(jnp.where(r == c, u, 0.0), axis=1, keepdims=True)
+    root = 1.0 / jnp.sqrt(d)
+    return jnp.where(c >= r, u, 0.0) * root, w * root
+
+
+def finish_kernel(gram, flat, basis, factor):
+    unit = 1.0 / BEAMS**0.5
+    r11, m11 = factor_half(gram[:128, :128])
+    factor[:128, :128] = r11 * unit
+    r12 = mm(m11, gram[:128, 128:])
+    factor[:128, 128:] = r12 * unit
+    factor[128:, :128] = jnp.zeros((128, 128), F32)
+    r22, m22 = factor_half(gram[128:, 128:] - mm(r12, r12, 0, 0))
+    factor[128:, 128:] = r22 * unit
+    up = BEAMS**0.5
+    left = mm(flat[:, :128], m11, 1, 1)
+    basis[:, :128] = left * up
+    basis[:, 128:] = mm(flat[:, 128:] - mm(left, r12), m22 * up, 1, 1)
+
+
+def finish(gram, flat):
+    vmem = pl.BlockSpec(memory_space=pltpu.VMEM)
+    return pl.pallas_call(
+        finish_kernel,
+        out_shape=(
+            jax.ShapeDtypeStruct((512, 256), F32),
+            jax.ShapeDtypeStruct((256, 256), F32),
+        ),
+        in_specs=[vmem, vmem],
+        out_specs=(vmem, vmem),
+        compiler_params=pltpu.CompilerParams(vmem_limit_bytes=24 * MIB),
+        name="finish",
+    )(gram, flat)
+
 
 def local(sketch, gains, coverage):
     rounded = pixel_pass(sketch, gains, coverage)
     total = beam_pass(coverage, gains, rounded)
     flat, gram = sum_pass(total.reshape(4, 4, 2, 512, 256))
-    lower = jnp.linalg.cholesky(gram)
-    solved = jax.scipy.linalg.solve_triangular(lower, flat.T, lower=True).T
-    scale = jnp.sqrt(jnp.float32(BEAMS))
-    return ((solved * scale).reshape(sketch.shape), lower.T / scale)
+    basis, factor = finish(gram, flat)
+    return basis.reshape(sketch.shape), factor
 
 
 def solution(mesh):

time: 290 us -> 240 us (0.83)
  other arithmetic: 54 us -> 0 us
  Pallas kernels: 222 us -> 235 us
  local copies, waits for them, and re-layouts: 9.41 us -> 4.1 us
    another operation x8 -> x0, other arithmetic: 53.9 us -> none  [the longest x6 34 us: local(): lower = jnp.linalg.cholesky(gram)]
    pallas_call x0 -> x1, Pallas kernels: none -> 12.8 us  [finish(): pl.pallas_call(finish_kernel, out_shape=(jax.ShapeDtypeStruct((512, 256),...]
    another operation x9 -> x0, local copies, waits for them, and re-layouts: 4.16 us -> none
where the time goes in v3:
time: 240 us; the launch traced here: 239 us
  Pallas kernels  235 us (98%)
  local copies, waits for them, and re-layouts  4.1 us (2%)
    pallas_call x1, Pallas kernels, pixel_pass(): pl.pallas_call(pixel_kernel, out_shape=jax.ShapeDtypeStruct((64, 128, 256...  119 us
    pallas_call x1, Pallas kernels, sum_pass(): pl.pallas_call(sum_kernel, out_shape=(jax.ShapeDtypeStruct((512, 256), F3...  78 us
    pallas_call x1, Pallas kernels, beam_pass(): pl.pallas_call(beam_kernel, grid_spec=spec, out_shape=jax.ShapeDtypeStruc...  25.4 us
    pallas_call x1, Pallas kernels, finish(): pl.pallas_call(finish_kernel, out_shape=(jax.ShapeDtypeStruct((512, 256),...  12.8 us

profile of v3, /device:TPU:1, one launch (start us, length us, event | category | flops | bytes accessed | tf_op | source)
XLA Modules:
  0.0 239.5 jit_solution(15215235837397778122)
XLA Ops:
  0.6 0.8 copy.5
  1.4 0.7 reshape.17.cov
  2.1 1.7 reshape.18.sk
  3.8 118.5 %pixel_pass.1.zb = bf16[64,128,256]{2,1,0:T(8,128)(2,1)} custom-call(s32[512]{0:T(512)} %reshape.17.cov, bf16[512,256]{1,0:T(8,128)(2,1)} %reshape.18.sk, bf16[64,8,128,128]{3,2,1,0:T(8,128)(2,1)} %g.1), custom_call_target="tpu_custom_call" | custom-call | flops 6499999744 | bytes 22000000 | tf_op jit(solution)/shard_map/pixel_pass/pallas_call | solution.py:272
  122.3 25.4 %beam_pass.1 = f32[16,2,512,256]{3,2,1,0:T(8,128)} custom-call(s32[512]{0:T(512)} %reshape.17.cov, bf16[64,8,128,128]{3,2,1,0:T(8,128)(2,1)} %g.1, bf16[64,128,256]{2,1,0:T(8,128)(2,1)} %pixel_pass.1.zb), custom_call_target="tpu_custom_call" | custom-call | flops 4300000256 | bytes 38000000 | tf_op jit(solution)/shard_map/beam_pass/pallas_call | solution.py:356
  147.7 78.0 %sum_pass.1 = (f32[512,256]{1,0:T(8,128)S(1)}, f32[256,256]{1,0:T(8,128)S(1)}) custom-call(f32[4,4,2,512,256]{4,3,2,1,0:T(8,128)} %bitcast.1), custom_call_target="tpu_custom_call" | custom-call | flops 500000000 | bytes 18000000 | tf_op jit(solution)/shard_map/sum_pass/pallas_call | solution.py:574
  225.7 12.8 %finish.1 = (f32[512,256]{1,0:T(8,128)S(1)}, f32[256,256]{1,0:T(8,128)}) custom-call(f32[256,256]{1,0:T(8,128)S(1)} %get-tuple-element.6.gram, f32[512,256]{1,0:T(8,128)S(1)} %get-tuple-element.7.flat), custom_call_target="tpu_custom_call" | custom-call | tf_op jit(solution)/shard_map/finish/pallas_call | solution.py:665
  238.5 0.9 reshape.20

commit v4 on v3

--- a/solution.py
+++ b/solution.py
@@ -12,6 +12,9 @@
 F32 = jnp.float32
 MESH = pl.DeviceIdType.MESH
 MIB = 1 << 20
+
+
+PLANE = [(n // 4, n % 4) for n in range(1, 16)]
 
 
 def place():
@@ -41,9 +44,11 @@
         sib=at(z, x, 1 - core),
         yr=(pix, step4(y, 1)),
         yl=(pix, step4(y, 3)),
-        xo=at(z, step4(x, 2), core),
-        zo=at(step4(z, 2), x, core),
         yo=(pix, step4(y, 2)),
+        **{
+            "p%d" % n: at(step4(z, dz), step4(x, dx), core)
+            for n, (dz, dx) in enumerate(PLANE)
+        },
     )
 
 
@@ -143,7 +148,7 @@
     from_row = ((o % 64) // 4) * 16 + (o // 64) * 4 + o % 4
     swap = (c == from_row).astype(F32).astype(BF)
 
-    @pl.loop(0, 32)
+    @pl.loop(0, 32, unroll=4)
     def _(q):
         for g in range(2):
             part = raw[pl.ds(2 * g, 2), :, :, pl.ds(pl.multiple_of(16 * q, 16), 16), :]
@@ -189,7 +194,7 @@
         def _():
             load(tau).wait()
 
-            @pl.loop(0, 8)
+            @pl.loop(0, 8, unroll=4)
             def _(tt):
                 t = tau * 8 + tt
                 lhs = jnp.concatenate([gbuf[t, s] for s in range(8)], axis=1)
@@ -289,7 +294,7 @@
     )(coverage.reshape(-1), sketch.reshape(512, 256), gains)
 
 
-TILES_STEP = 4
+TILES_STEP = 16
 
 
 def beam_kernel(cov, g, zb, out, acc, split, sems):
@@ -301,7 +306,8 @@
         def _(b):
             acc[b] = jnp.zeros((128, 256), F32)
 
-    for tt in range(TILES_STEP):
+    @pl.loop(0, TILES_STEP, unroll=4)
+    def _(tt):
         rows = zb[tt]
         for s in range(8):
             b = cov[(step * TILES_STEP + tt) * 8 + s]
@@ -370,7 +376,7 @@
 
 
 def sum_kernel(
-    part, flat, gram, own, sib, got1, got2, gacc, gout, gsib, gx, gz, gy,
+    part, flat, gram, own, sib, got1, got2, gacc, gout, gsib, gz, gy,
     csend, crecv, rsend, rrecv, gsend, grecv, local,
 ):
     pix, y, z, x, core = place()
@@ -395,7 +401,8 @@
     for j in range(SUB):
         for h in range(2):
             load(h, j).start()
-    greet(("xr", "xl", "zr", "zl", "sib", "yr", "yl", "xo", "zo", "yo"), near)
+    plane = tuple("p%d" % n for n in range(15))
+    greet(plane + ("sib", "yr", "yl", "yo"), near)
     for j in range(SUB):
         for h in range(2):
             swap(h, j).start()
@@ -516,28 +523,25 @@
     exchange(0, [(block(128 * other, 128), gsib, "sib")])
     mine = block(base, 128)
     mine[...] += gsib[...]
-    xat = base + 32 * x
+    def spot(n):
+        dz, dx = PLANE[n]
+        return base + 8 * (4 * step4(z, dz) + step4(x, dx))
+
     exchange(1, [
-        (block(base + 32 * step4(x, d), 32), gx.at[d - 1], to)
-        for d, to in ((1, "xr"), (2, "xo"), (3, "xl"))
+        (block(spot(n), 8), gz.at[n], "p%d" % n) for n in range(15)
     ])
-    mine = block(xat, 32)
-    mine[...] += gx[0] + gx[1] + gx[2]
-    zat = xat + 8 * z
-    exchange(4, [
-        (block(xat + 8 * step4(z, d), 8), gz.at[d - 1], to)
-        for d, to in ((1, "zr"), (2, "zo"), (3, "zl"))
-    ])
-    mine = block(zat, 8)
-    gy[y] = mine[...] + (gz[0] + gz[1] + gz[2])
-    exchange(7, [(gy.at[y], gy.at[y], to) for to in ("yr", "yo", "yl")])
-    mine = block(zat, 8, gout)
+    at = base + 8 * (4 * z + x)
+    mine = block(at, 8)
+    total = mine[...]
+    for n in range(15):
+        total = total + gz[n]
+    gy[y] = total
+    exchange(16, [(gy.at[y], gy.at[y], to) for to in ("yr", "yo", "yl")])
+    mine = block(at, 8, gout)
     mine[...] = (gy[0] + gy[1]) + (gy[2] + gy[3])
-    exchange(10, [(mine, mine, to) for to in ("zr", "zo", "zl")])
-    mine = block(xat, 32, gout)
-    exchange(13, [(mine, mine, to) for to in ("xr", "xo", "xl")])
+    exchange(19, [(mine, mine, "p%d" % n) for n in range(15)])
     mine = block(base, 128, gout)
-    exchange(16, [(mine, mine, "sib")])
+    exchange(34, [(mine, mine, "sib")])
     gram[...] = gout[...]
     for m in sent:
         m.wait_send()
@@ -560,15 +564,14 @@
         pltpu.VMEM((256, 256), F32),
         pltpu.VMEM((256, 256), F32),
         pltpu.VMEM((128, 256), F32),
-        pltpu.VMEM((3, 32, 256), F32),
-        pltpu.VMEM((3, 8, 256), F32),
+        pltpu.VMEM((15, 8, 256), F32),
         pltpu.VMEM((4, 8, 256), F32),
         pltpu.SemaphoreType.DMA((2, SUB)),
         pltpu.SemaphoreType.DMA((2, SUB)),
         pltpu.SemaphoreType.DMA((2, SUB, 2, 6)),
         pltpu.SemaphoreType.DMA((2, SUB, 2, 6)),
-        pltpu.SemaphoreType.DMA((17,)),
-        pltpu.SemaphoreType.DMA((17,)),
+        pltpu.SemaphoreType.DMA((35,)),
+        pltpu.SemaphoreType.DMA((35,)),
         pltpu.SemaphoreType.DMA((2, SUB)),
     ]
     return pl.pallas_call(

time: 240 us -> 228 us (0.950)
  Pallas kernels: 235 us -> 223 us
    pallas_call x1, Pallas kernels: 119 us -> 114 us  [pixel_pass(): pl.pallas_call(pixel_kernel, out_shape=jax.ShapeDtypeStruct((64, 128, 256...]
    pallas_call x1, Pallas kernels: 78 us -> 74.2 us  [sum_pass(): pl.pallas_call(sum_kernel, out_shape=(jax.ShapeDtypeStruct((512, 256), F3...]
    pallas_call x1, Pallas kernels: 25.4 us -> 22.4 us  [beam_pass(): pl.pallas_call(beam_kernel, grid_spec=spec, out_shape=jax.ShapeDtypeStruc...]
where the time goes in v4:
time: 228 us
  Pallas kernels  223 us (98%)
  local copies, waits for them, and re-layouts  4.1 us (2%)
    pallas_call x1, Pallas kernels, pixel_pass(): pl.pallas_call(pixel_kernel, out_shape=jax.ShapeDtypeStruct((64, 128, 256...  114 us
    pallas_call x1, Pallas kernels, sum_pass(): pl.pallas_call(sum_kernel, out_shape=(jax.ShapeDtypeStruct((512, 256), F3...  74.2 us
    pallas_call x1, Pallas kernels, beam_pass(): pl.pallas_call(beam_kernel, grid_spec=spec, out_shape=jax.ShapeDtypeStruc...  22.4 us
    pallas_call x1, Pallas kernels, finish(): pl.pallas_call(finish_kernel, out_shape=(jax.ShapeDtypeStruct((512, 256),...  12.8 us

profile of v4, /device:TPU:1, one launch (start us, length us, event | category | flops | bytes accessed | tf_op | source)
XLA Modules:
  0.0 227.7 jit_solution(6269729123680633019)
XLA Ops:
  0.6 0.8 copy.5
  1.4 0.7 reshape.17.cov
  2.1 1.7 reshape.18.sk
  3.8 113.5 %pixel_pass.1.zb = bf16[64,128,256]{2,1,0:T(8,128)(2,1)} custom-call(s32[512]{0:T(512)} %reshape.17.cov, bf16[512,256]{1,0:T(8,128)(2,1)} %reshape.18.sk, bf16[64,8,128,128]{3,2,1,0:T(8,128)(2,1)} %g.1), custom_call_target="tpu_custom_call" | custom-call | flops 6499999744 | bytes 22000000 | tf_op jit(solution)/shard_map/pixel_pass/pallas_call | solution.py:277
  117.3 22.4 %beam_pass.1 = f32[16,2,512,256]{3,2,1,0:T(8,128)} custom-call(s32[512]{0:T(512)} %reshape.17.cov, bf16[64,8,128,128]{3,2,1,0:T(8,128)(2,1)} %g.1, bf16[64,128,256]{2,1,0:T(8,128)(2,1)} %pixel_pass.1.zb), custom_call_target="tpu_custom_call" | custom-call | flops 4300000256 | bytes 38000000 | tf_op jit(solution)/shard_map/beam_pass/pallas_call | solution.py:362
  139.7 74.2 %sum_pass.1 = (f32[512,256]{1,0:T(8,128)S(1)}, f32[256,256]{1,0:T(8,128)S(1)}) custom-call(f32[4,4,2,512,256]{4,3,2,1,0:T(8,128)} %bitcast.1), custom_call_target="tpu_custom_call" | custom-call | flops 500000000 | bytes 18000000 | tf_op jit(solution)/shard_map/sum_pass/pallas_call | solution.py:577
  214.0 12.8 %finish.1 = (f32[512,256]{1,0:T(8,128)S(1)}, f32[256,256]{1,0:T(8,128)}) custom-call(f32[256,256]{1,0:T(8,128)S(1)} %get-tuple-element.6.gram, f32[512,256]{1,0:T(8,128)S(1)} %get-tuple-element.7.flat), custom_call_target="tpu_custom_call" | custom-call | tf_op jit(solution)/shard_map/finish/pallas_call | solution.py:668
  226.8 0.9 reshape.20

commit v5 on v4

v5 whole, which is shorter than its diff:
```python
import functools

import jax
import jax.numpy as jnp
from jax import lax
from jax.experimental import pallas as pl
from jax.experimental.pallas import tpu as pltpu
from jax.sharding import PartitionSpec as P

BEAMS = 65536
BF = jnp.bfloat16
F32 = jnp.float32
MESH = pl.DeviceIdType.MESH
MIB = 1 << 20


PLANE = [(n // 4, n % 4) for n in range(1, 16)]


def place():
    pix = lax.axis_index("pix")
    y = lax.axis_index("beam")
    core = lax.rem(pix, 2)
    x = lax.rem(lax.div(pix, 2), 4)
    z = lax.div(pix, 8)
    return pix, y, z, x, core


def step4(v, d):
    return lax.rem(v + d, 4)


def neighbours():
    pix, y, z, x, core = place()

    def at(zz, xx, cc):
        return ((zz * 4 + xx) * 2 + cc, y)

    return dict(
        xr=at(z, step4(x, 1), core),
        xl=at(z, step4(x, 3), core),
        zr=at(step4(z, 1), x, core),
        zl=at(step4(z, 3), x, core),
        sib=at(z, x, 1 - core),
        yr=(pix, step4(y, 1)),
        yl=(pix, step4(y, 3)),
        yo=(pix, step4(y, 2)),
        **{
            "p%d" % n: at(step4(z, dz), step4(x, dx), core)
            for n, (dz, dx) in enumerate(PLANE)
        },
    )


def greet(names, near):
    barrier = pltpu.get_barrier_semaphore()
    for name in names:
        pl.semaphore_signal(barrier, inc=1, device_id=near[name], device_id_type=MESH)
    pl.semaphore_wait(barrier, len(names))


W = 128
CHUNKS = 4
TC = 64 // CHUNKS
PART = TC // 8


def gatherer(sk, raw, gsend, grecv, local):
    pix, y, z, x, core = place()
    near = neighbours()
    lo, hi = pl.ds(0, 256), pl.ds(256, 256)
    xm, xp, xo = step4(x, 3), step4(x, 1), step4(x, 2)
    zm, zp, zo = step4(z, 3), step4(z, 1), step4(z, 2)
    row = (z, slice(None), core, lo)
    col = (slice(None), x, core, hi)
    table = (
        ((z, x, core, lo), "xr"),
        ((z, x, core, lo), "xl"),
        ((z, x, core, hi), "zr"),
        ((z, x, core, hi), "zl"),
        ((z, xm, core, pl.ds(0, 128)), "xr"),
        ((z, xp, core, pl.ds(128, 128)), "xl"),
        ((zm, x, core, pl.ds(256, 128)), "zr"),
        ((zp, x, core, pl.ds(384, 128)), "zl"),
        (row, "zr"),
        (row, "zl"),
        (col, "xr"),
        (col, "xl"),
        (row, "sib"),
        (col, "sib"),
        ((zm, pl.ds(0, 2), core, lo), "zr"),
        ((zp, pl.ds(2, 2), core, lo), "zl"),
        ((pl.ds(0, 2), xm, core, hi), "xr"),
        ((pl.ds(2, 2), xp, core, hi), "xl"),
        ((zm, slice(None), core, lo), "sib"),
        ((zp, slice(None), core, lo), "sib"),
        ((slice(None), xm, core, hi), "sib"),
        ((slice(None), xp, core, hi), "sib"),
        ((zo, slice(None), core, lo), "sib"),
        ((slice(None), xo, core, hi), "sib"),
    )

    def cp(k):
        at, to = table[k]
        return pltpu.make_async_remote_copy(
            src_ref=raw.at[at], dst_ref=raw.at[at],
            send_sem=gsend.at[k], recv_sem=grecv.at[k],
            device_id=near[to], device_id_type=MESH,
        )

    def load():
        return pltpu.make_async_copy(sk, raw.at[z, x, core], local)

    def pairs(*steps):
        for wait, start in steps:
            for k in wait:
                cp(k).wait_recv()
            for k in start:
                cp(k).start()

    def begin():
        load().wait()
        pairs(((), (0, 1, 2, 3)))

    def relay():
        pairs(((0,), (4,)), ((1,), (5,)), ((2,), (6,)), ((3,), (7,)))

    def second():
        pairs(((4, 5), (8, 9)), ((6, 7), (10, 11, 12, 13)))

    def relay2():
        pairs(
            ((8,), (14,)), ((9,), (15,)), ((10,), (16,)),
            ((11,), (17, 18, 19, 20, 21)),
        )

    def last():
        pairs(((14, 15), (22,)), ((16, 17), (23,)))

    def done():
        pairs(((12, 13, 18, 19, 20, 21, 22, 23), ()))

    def close():
        for k in range(24):
            cp(k).wait_send()

    return load, (begin, relay, second, relay2, last, done), close


def regroup(raw, om):
    o = lax.broadcasted_iota(jnp.int32, (256, 256), 0)
    c = lax.broadcasted_iota(jnp.int32, (256, 256), 1)
    from_row = ((o % 64) // 4) * 16 + (o // 64) * 4 + o % 4
    swap = (c == from_row).astype(F32).astype(BF)

    @pl.loop(0, 32, unroll=4)
    def _(q):
        for g in range(2):
            part = raw[pl.ds(2 * g, 2), :, :, pl.ds(pl.multiple_of(16 * q, 16), 16), :]
            part = part.reshape(256, W)
            turned = jnp.dot(swap, part, preferred_element_type=F32).astype(BF)
            om[pl.ds(4 * q, 4), pl.ds(64 * g, 64), :] = turned.reshape(4, 64, W)


def pixel_sums(cov, om, gains, out, gbuf, zf, zs, zb, got, csend, bsend, brecv, local):
    y = lax.axis_index("beam")
    near = neighbours()
    c0, c1, c2, c3 = y, step4(y, 1), step4(y, 2), step4(y, 3)

    def rc(k, i, src, dst, to):
        return pltpu.make_async_remote_copy(
            src_ref=src, dst_ref=dst, send_sem=bsend.at[k, i], recv_sem=brecv.at[k, i],
            device_id=near[to], device_id_type=MESH,
        )

    def lo(i, c):
        return pl.ds(TC * i + 2 * PART * c, PART)

    def hi(i, c):
        return pl.ds(TC * i + 2 * PART * c + PART, PART)

    def copies(i):
        own = zb.at[pl.ds(TC * i + 2 * PART * c0, 2 * PART)]
        left = zb.at[lo(i, c3)]
        right = zb.at[hi(i, c1)]
        table = (
            (zs.at[lo(i, c2)], got.at[0, i], "yr"),
            (zs.at[hi(i, c1)], got.at[1, i], "yr"),
            (zs.at[hi(i, c2)], got.at[2, i], "yl"),
            (zs.at[lo(i, c3)], got.at[3, i], "yl"),
            (csend.at[0, i], got.at[4, i], "yr"),
            (csend.at[1, i], got.at[5, i], "yl"),
            (own, own, "yr"),
            (own, own, "yl"),
            (left, left, "yr"),
            (right, right, "yl"),
        )
        return lambda k: rc(k, i, *table[k])

    def store(i):
        at = pl.ds(TC * i, TC)
        return pltpu.make_async_copy(zb.at[at], out.at[at], local.at[CHUNKS + i])

    def load(i):
        at = pl.ds(TC * i, TC)
        return pltpu.make_async_copy(gains.at[at], gbuf.at[at], local.at[i])

    def begin(i):
        load(i).wait()

        @pl.loop(0, TC, unroll=4)
        def _(tt):
            t = i * TC + tt
            lhs = jnp.concatenate([gbuf[t, s] for s in range(8)], axis=1)
            rhs = jnp.concatenate([om[cov[t * 8 + s]] for s in range(8)], axis=0)
            acc = jnp.dot(lhs, rhs, preferred_element_type=F32)
            zf[t] = acc
            zs[t] = acc.astype(BF)

        m = copies(i)
        for k in range(4):
            m(k).start()

    def second(i):
        m = copies(i)
        m(0).wait_recv()
        csend[0, i] = (got[0, i].astype(F32) + zf[lo(i, c1)]).astype(BF)
        m(4).start()
        m(2).wait_recv()
        csend[1, i] = (got[2, i].astype(F32) + zf[hi(i, c3)]).astype(BF)
        m(5).start()

    def third(i):
        m = copies(i)
        m(3).wait_recv()
        m(4).wait_recv()
        a = zf[lo(i, c0)] + got[3, i].astype(F32) + got[4, i].astype(F32)
        zb[lo(i, c0)] = a.astype(BF)
        m(1).wait_recv()
        m(5).wait_recv()
        a = zf[hi(i, c0)] + got[1, i].astype(F32) + got[5, i].astype(F32)
        zb[hi(i, c0)] = a.astype(BF)
        m(6).start()
        m(7).start()

    def fourth(i):
        m = copies(i)
        m(6).wait_recv()
        m(8).start()
        m(7).wait_recv()
        m(9).start()

    def fifth(i):
        m = copies(i)
        m(8).wait_recv()
        m(9).wait_recv()
        store(i).start()

    def sixth(i):
        m = copies(i)
        for k in range(10):
            m(k).wait_send()
        store(i).wait()

    def start_loads():
        for i in range(CHUNKS):
            load(i).start()

    return start_loads, (begin, second, third, fourth, fifth, sixth)


def run_stages(tau, stages, count, after=0):
    for n, work in enumerate(stages):

        @pl.when(jnp.logical_and(tau >= after + n, tau < after + n + count))
        def _():
            work(tau - after - n)


PIXEL_SCRATCH = [
    pltpu.VMEM((64, 8, 128, 128), BF),
    pltpu.VMEM((64, 128, W), F32),
    pltpu.VMEM((64, 128, W), BF),
    pltpu.VMEM((64, 128, W), BF),
    pltpu.VMEM((6, CHUNKS, PART, 128, W), BF),
    pltpu.VMEM((2, CHUNKS, PART, 128, W), BF),
    pltpu.SemaphoreType.DMA((10, CHUNKS)),
    pltpu.SemaphoreType.DMA((10, CHUNKS)),
    pltpu.SemaphoreType.DMA((2 * CHUNKS,)),
]


def first_kernel(cov, sk, gains, out, om_out, raw, om, gsend, grecv, local, *rest):
    near = neighbours()
    parts = [
        gatherer(sk.at[h], raw.at[h], gsend.at[h], grecv.at[h], local.at[h])
        for h in range(2)
    ]
    start_loads, stages = pixel_sums(cov, om.at[0], gains, out, *rest)
    parts[0][0]().start()
    parts[1][0]().start()
    greet(("xr", "xl", "zr", "zl", "sib", "yr", "yl"), near)
    steps = parts[0][1]
    steps[0]()
    start_loads()
    for step in steps[1:]:
        step()
    later = parts[1][1]
    later[0]()
    regroup(raw.at[0], om.at[0])

    def keep():
        return pltpu.make_async_copy(om.at[1], om_out, local.at[2])

    @pl.loop(0, CHUNKS + 5)
    def _(tau):
        run_stages(tau, stages, CHUNKS)
        for step, at in zip(later[1:], GATHER_AT):

            @pl.when(tau == at)
            def _():
                step()

        @pl.when(tau == GATHER_AT[-1])
        def _():
            regroup(raw.at[1], om.at[1])
            keep().start()

    for part in parts:
        part[2]()
    keep().wait()


GATHER_AT = (0, 1, 2, 3, 4)


def first_pass(sketch, gains, coverage):
    scratch = [
        pltpu.VMEM((2, 4, 4, 2, 512, W), BF),
        pltpu.VMEM((2, 128, 128, W), BF),
        pltpu.SemaphoreType.DMA((2, 24)),
        pltpu.SemaphoreType.DMA((2, 24)),
        pltpu.SemaphoreType.DMA((3,)),
        *PIXEL_SCRATCH,
    ]
    hbm = pl.BlockSpec(memory_space=pl.ANY)
    return pl.pallas_call(
        first_kernel,
        out_shape=(
            jax.ShapeDtypeStruct((64, 128, W), BF),
            jax.ShapeDtypeStruct((128, 128, W), BF),
        ),
        in_specs=[pl.BlockSpec(memory_space=pltpu.SMEM), hbm, hbm],
        out_specs=(hbm, hbm),
        scratch_shapes=scratch,
        compiler_params=pltpu.CompilerParams(
            collective_id=0, has_side_effects=True, vmem_limit_bytes=60 * MIB
        ),
        cost_estimate=pl.CostEstimate(
            flops=4_400_000_000, bytes_accessed=24_000_000, transcendentals=0
        ),
        name="first_pass",
    )(coverage.reshape(-1), sketch, gains)


TILES_STEP = 16


def beam_kernel(cov, g, zb, out, acc, split, sems):
    step = pl.program_id(0)

    @pl.when(step == 0)
    def _():
        @pl.loop(0, 128)
        def _(b):
            acc[b] = jnp.zeros((128, W), F32)

    @pl.loop(0, TILES_STEP, unroll=4)
    def _(tt):
        rows = zb[tt]
        for s in range(8):
            b = cov[(step * TILES_STEP + tt) * 8 + s]
            acc[b] += lax.dot_general(
                g[tt, s], rows, (((0,), (0,)), ((), ())), preferred_element_type=F32
            )

    @pl.when(step == pl.num_programs(0) - 1)
    def _():
        low = lax.broadcasted_iota(jnp.int32, (16, 8, W), 1) < 4

        def store(i):
            return pltpu.make_async_copy(
                split.at[:, :, pl.ds(pl.multiple_of(64 * i, 64), 64)],
                out.at[:, :, pl.ds(pl.multiple_of(64 * i, 64), 64)],
                sems.at[i],
            )

        @pl.loop(0, 8)
        def _(i):
            @pl.loop(0, 8)
            def _(j):
                pair = i * 8 + j
                a = acc[2 * pair].reshape(16, 8, W)
                b = acc[2 * pair + 1].reshape(16, 8, W)
                at = pl.ds(pl.multiple_of(8 * pair, 8), 8)
                split[:, 0, at, :] = jnp.where(low, a, pltpu.roll(b, 4, 1))
                split[:, 1, at, :] = jnp.where(low, pltpu.roll(a, 4, 1), b)

            store(i).start()

        @pl.loop(0, 8)
        def _(i):
            store(i).wait()


def beam_pass(coverage, gains, rounded):
    spec = pltpu.PrefetchScalarGridSpec(
        num_scalar_prefetch=1,
        grid=(64 // TILES_STEP,),
        in_specs=[
            pl.BlockSpec((TILES_STEP, 8, 128, 128), lambda i, c: (i, 0, 0, 0)),
            pl.BlockSpec((TILES_STEP, 128, W), lambda i, c: (i, 0, 0)),
        ],
        out_specs=pl.BlockSpec(memory_space=pl.ANY),
        scratch_shapes=[
            pltpu.VMEM((128, 128, W), F32),
            pltpu.VMEM((16, 2, 512, W), F32),
            pltpu.SemaphoreType.DMA((8,)),
        ],
    )
    return pl.pallas_call(
        beam_kernel,
        grid_spec=spec,
        out_shape=jax.ShapeDtypeStruct((16, 2, 512, W), F32),
        compiler_params=pltpu.CompilerParams(vmem_limit_bytes=56 * MIB),
        cost_estimate=pl.CostEstimate(
            flops=4_300_000_000, bytes_accessed=38_000_000, transcendentals=0
        ),
        name="beam_pass",
    )(coverage.reshape(-1), gains, rounded)

SUB = 4
ROWS = 256 // SUB
HALF = ROWS // 2


def row_sums(part, flat, at, own, sib, got1, got2, csend, crecv, rsend, rrecv, local):
    pix, y, z, x, core = place()
    near = neighbours()
    other = 1 - core

    def rows(h, j):
        return pl.ds(pl.multiple_of(256 * h + ROWS * j, ROWS), ROWS)

    def load(h, j):
        return pltpu.make_async_copy(
            part.at[:, :, core, rows(h, j)], own.at[h, j], local.at[h, j]
        )

    def swap(h, j):
        return pltpu.make_async_remote_copy(
            src_ref=part.at[:, :, other, rows(h, j)], dst_ref=sib.at[h, j],
            send_sem=csend.at[h, j], recv_sem=crecv.at[h, j],
            device_id=near["sib"], device_id_type=MESH,
        )

    def start_loads():
        for j in range(SUB):
            for h in range(2):
                load(h, j).start()

    def start_swaps():
        for j in range(SUB):
            for h in range(2):
                swap(h, j).start()

    def ring(h, phase):
        if (h == 0) == (phase == 0):
            return x, "xr", "xl"
        return z, "zr", "zl"

    def piece(h, j, phase, d, lo):
        if phase == 0:
            two = pl.ds(0 if lo else 2, 2)
            return own.at[h, j, two, d] if h == 0 else own.at[h, j, d, two]
        n = pl.ds(0 if lo else HALF, HALF)
        return own.at[h, j, d, x, n] if h == 0 else own.at[h, j, z, d, n]

    def msg(h, j, phase, k):
        c, right, left = ring(h, phase)
        got = got1 if phase == 0 else got2
        d, lo, to = (
            (step4(c, 2), True, right),
            (step4(c, 1), False, right),
            (step4(c, 2), False, left),
            (step4(c, 3), True, left),
            (step4(c, 1), True, right),
            (step4(c, 3), False, left),
        )[k]
        return pltpu.make_async_remote_copy(
            src_ref=piece(h, j, phase, d, lo), dst_ref=got.at[h, j, k],
            send_sem=rsend.at[h, j, phase, k], recv_sem=rrecv.at[h, j, phase, k],
            device_id=near[to], device_id_type=MESH,
        )

    def first(h, j, phase):
        for k in range(4):
            msg(h, j, phase, k).start()

    def second(h, j, phase):
        c = ring(h, phase)[0]
        got = got1 if phase == 0 else got2
        msg(h, j, phase, 0).wait_recv()
        mid = piece(h, j, phase, step4(c, 1), True)
        mid[...] += got[h, j, 0]
        msg(h, j, phase, 4).start()
        msg(h, j, phase, 2).wait_recv()
        mid = piece(h, j, phase, step4(c, 3), False)
        mid[...] += got[h, j, 2]
        msg(h, j, phase, 5).start()

    def finish(h, j, phase):
        c = ring(h, phase)[0]
        got = got1 if phase == 0 else got2
        for k in (3, 4, 1, 5):
            msg(h, j, phase, k).wait_recv()
        lo = piece(h, j, phase, c, True)
        lo[...] += got[h, j, 3] + got[h, j, 4]
        hi = piece(h, j, phase, c, False)
        hi[...] += got[h, j, 1] + got[h, j, 5]

    def both(work):
        def run(j):
            for h in range(2):
                work(h, j)

        return run

    def begin(h, j):
        load(h, j).wait()
        swap(h, j).wait_recv()

        @pl.loop(0, 4)
        def _(i):
            own[h, j, i] += sib[h, j, i]

        first(h, j, 0)

    def turn(h, j):
        finish(h, j, 0)
        first(h, j, 1)

    def end(h, j):
        finish(h, j, 1)
        flat[rows(h, j), at] = own[h, j, z, x]

    def settle(h, j):
        swap(h, j).wait_send()
        for phase in range(2):
            for k in range(6):
                msg(h, j, phase, k).wait_send()

    stages = (
        both(begin),
        both(lambda h, j: second(h, j, 0)),
        both(turn),
        both(lambda h, j: second(h, j, 1)),
        both(end),
        both(settle),
    )

    return start_loads, start_swaps, stages


SUM_SCRATCH = [
    pltpu.VMEM((2, SUB, 4, 4, ROWS, W), F32),
    pltpu.VMEM((2, SUB, 4, 4, ROWS, W), F32),
    pltpu.VMEM((2, SUB, 6, 2, ROWS, W), F32),
    pltpu.VMEM((2, SUB, 6, HALF, W), F32),
    pltpu.SemaphoreType.DMA((2, SUB)),
    pltpu.SemaphoreType.DMA((2, SUB)),
    pltpu.SemaphoreType.DMA((2, SUB, 2, 6)),
    pltpu.SemaphoreType.DMA((2, SUB, 2, 6)),
    pltpu.SemaphoreType.DMA((2, SUB)),
]


def second_kernel(cov, om_in, gains, part, out, flat, om, local, *rest):
    near = neighbours()
    n = len(PIXEL_SCRATCH)
    start_gains, pixel = pixel_sums(cov, om, gains, out, *rest[:n])
    start_own, start_swaps, rows = row_sums(
        part, flat, slice(None), *rest[n:]
    )
    fetch = pltpu.make_async_copy(om_in, om, local)
    fetch.start()
    start_gains()
    start_own()
    greet(("xr", "xl", "zr", "zl", "sib", "yr", "yl"), near)
    start_swaps()
    fetch.wait()

    @pl.loop(0, max(CHUNKS, SUB) + 5)
    def _(tau):
        for n in range(6):
            run_stages(tau, pixel[n : n + 1], CHUNKS, n)
            run_stages(tau, rows[n : n + 1], SUB, n)


def second_pass(coverage, om, gains, part):
    hbm = pl.BlockSpec(memory_space=pl.ANY)
    return pl.pallas_call(
        second_kernel,
        out_shape=(
            jax.ShapeDtypeStruct((64, 128, W), BF),
            jax.ShapeDtypeStruct((512, W), F32),
        ),
        in_specs=[pl.BlockSpec(memory_space=pltpu.SMEM), hbm, hbm, hbm],
        out_specs=(hbm, pl.BlockSpec(memory_space=pltpu.VMEM)),
        scratch_shapes=[
            pltpu.VMEM((128, 128, W), BF),
            pltpu.SemaphoreType.DMA,
            *PIXEL_SCRATCH,
            *SUM_SCRATCH,
        ],
        compiler_params=pltpu.CompilerParams(
            collective_id=1, has_side_effects=True, vmem_limit_bytes=60 * MIB
        ),
        cost_estimate=pl.CostEstimate(
            flops=2_200_000_000, bytes_accessed=32_000_000, transcendentals=0
        ),
        name="second_pass",
    )(coverage.reshape(-1), om, gains, part)


def third_kernel(
    part, flat0, flat, gram, gacc, gout, gsib, gz, gy, gsend, grecv, *rest
):
    pix, y, z, x, core = place()
    near = neighbours()
    other = 1 - core
    start_own, start_swaps, stages = row_sums(part, flat, pl.ds(W, W), *rest)
    start_own()
    plane = tuple("p%d" % n for n in range(15))
    greet(plane + ("sib", "yr", "yl", "yo"), near)
    start_swaps()
    flat[:, :W] = flat0[...]

    @pl.loop(0, SUB + 5)
    def _(tau):
        run_stages(tau, stages, SUB)

    f = flat[...]
    gacc[...] = lax.dot_general(
        f, f, (((0,), (0,)), ((), ())),
        precision=lax.Precision.HIGHEST, preferred_element_type=F32,
    )

    def gmsg(k, src, dst, to):
        return pltpu.make_async_remote_copy(
            src_ref=src, dst_ref=dst, send_sem=gsend.at[k], recv_sem=grecv.at[k],
            device_id=near[to], device_id_type=MESH,
        )

    def block(at, n, ref=gacc):
        return ref.at[pl.ds(pl.multiple_of(at, n), n)]

    sent = []

    def exchange(k, pairs):
        todo = [gmsg(k + n, *p) for n, p in enumerate(pairs)]
        for m in todo:
            m.start()
        for m in todo:
            m.wait_recv()
        sent.extend(todo)

    base = 128 * core
    exchange(0, [(block(128 * other, 128), gsib, "sib")])
    mine = block(base, 128)
    mine[...] += gsib[...]
    def spot(n):
        dz, dx = PLANE[n]
        return base + 8 * (4 * step4(z, dz) + step4(x, dx))

    exchange(1, [
        (block(spot(n), 8), gz.at[n], "p%d" % n) for n in range(15)
    ])
    at = base + 8 * (4 * z + x)
    mine = block(at, 8)
    total = mine[...]
    for n in range(15):
        total = total + gz[n]
    gy[y] = total
    exchange(16, [(gy.at[y], gy.at[y], to) for to in ("yr", "yo", "yl")])
    mine = block(at, 8, gout)
    mine[...] = (gy[0] + gy[1]) + (gy[2] + gy[3])
    exchange(19, [(mine, mine, "p%d" % n) for n in range(15)])
    mine = block(base, 128, gout)
    exchange(34, [(mine, mine, "sib")])
    gram[...] = gout[...]
    for m in sent:
        m.wait_send()


def third_pass(part, flat0):
    vmem = pl.BlockSpec(memory_space=pltpu.VMEM)
    return pl.pallas_call(
        third_kernel,
        out_shape=(
            jax.ShapeDtypeStruct((512, 256), F32),
            jax.ShapeDtypeStruct((256, 256), F32),
        ),
        in_specs=[pl.BlockSpec(memory_space=pl.ANY), vmem],
        out_specs=(vmem, vmem),
        scratch_shapes=[
            pltpu.VMEM((256, 256), F32),
            pltpu.VMEM((256, 256), F32),
            pltpu.VMEM((128, 256), F32),
            pltpu.VMEM((15, 8, 256), F32),
            pltpu.VMEM((4, 8, 256), F32),
            pltpu.SemaphoreType.DMA((35,)),
            pltpu.SemaphoreType.DMA((35,)),
            *SUM_SCRATCH,
        ],
        compiler_params=pltpu.CompilerParams(
            collective_id=2, has_side_effects=True, vmem_limit_bytes=60 * MIB
        ),
        cost_estimate=pl.CostEstimate(
            flops=500_000_000, bytes_accessed=9_000_000, transcendentals=0
        ),
        name="third_pass",
    )(part, flat0)


PIVOTS = 4


def eliminate(a):
    sub = lax.broadcasted_iota(jnp.int32, (8, 128), 0)
    lane = lax.broadcasted_iota(jnp.int32, (8, 128), 1)
    rows = [a[8 * i : 8 * i + 8] for i in range(16)]
    inv = [(lane == sub + 8 * i).astype(F32) for i in range(16)]
    for start in range(0, 128, PIVOTS):
        g = start // 8
        cols = [
            [jnp.broadcast_to(r[:, j : j + 1], (8, 128)) for r in rows[g:]]
            for j in range(start, start + PIVOTS)
        ]
        for k in range(PIVOTS):
            at = start + k - 8 * g
            one = jnp.broadcast_to(cols[k][0][at : at + 1], (8, 128))
            scale = 1.0 / one
            head = jnp.broadcast_to(rows[g][at : at + 1], (8, 128))
            head_inv = jnp.broadcast_to(inv[g][at : at + 1], (8, 128))
            heads = [
                jnp.broadcast_to(cols[m][0][at : at + 1], (8, 128))
                for m in range(k + 1, PIVOTS)
            ]
            for i in range(g, 16):
                f = cols[k][i - g] * scale
                if i == g:
                    f = jnp.where(sub > at, f, 0.0)
                for n, m in enumerate(range(k + 1, PIVOTS)):
                    cols[m][i - g] = cols[m][i - g] - f * heads[n]
                rows[i] = rows[i] - f * head
                inv[i] = inv[i] - f * head_inv
    u = jnp.concatenate(rows, axis=0)
    w = jnp.concatenate(inv, axis=0)
    return u, w


def mm(a, b, ca=1, cb=0):
    return lax.dot_general(
        a, b, (((ca,), (cb,)), ((), ())),
        precision=lax.Precision.HIGHEST, preferred_element_type=F32,
    )


def factor_half(a):
    u, w = eliminate(a)
    r = lax.broadcasted_iota(jnp.int32, (128, 128), 0)
    c = lax.broadcasted_iota(jnp.int32, (128, 128), 1)
    d = jnp.sum(jnp.where(r == c, u, 0.0), axis=1, keepdims=True)
    root = 1.0 / jnp.sqrt(d)
    return jnp.where(c >= r, u, 0.0) * root, w * root


def finish_kernel(gram, flat, basis, factor):
    unit = 1.0 / BEAMS**0.5
    r11, m11 = factor_half(gram[:128, :128])
    factor[:128, :128] = r11 * unit
    r12 = mm(m11, gram[:128, 128:])
    factor[:128, 128:] = r12 * unit
    factor[128:, :128] = jnp.zeros((128, 128), F32)
    r22, m22 = factor_half(gram[128:, 128:] - mm(r12, r12, 0, 0))
    factor[128:, 128:] = r22 * unit
    up = BEAMS**0.5
    left = mm(flat[:, :128], m11, 1, 1)
    basis[:, :128] = left * up
    basis[:, 128:] = mm(flat[:, 128:] - mm(left, r12), m22 * up, 1, 1)


def finish(gram, flat):
    vmem = pl.BlockSpec(memory_space=pltpu.VMEM)
    return pl.pallas_call(
        finish_kernel,
        out_shape=(
            jax.ShapeDtypeStruct((512, 256), F32),
            jax.ShapeDtypeStruct((256, 256), F32),
        ),
        in_specs=[vmem, vmem],
        out_specs=(vmem, vmem),
        compiler_params=pltpu.CompilerParams(vmem_limit_bytes=24 * MIB),
        name="finish",
    )(gram, flat)


def local(sketch, gains, coverage):
    halves = sketch.reshape(512, 2, W).transpose(1, 0, 2)
    shape = (4, 4, 2, 512, W)
    rounded, omega = first_pass(halves, gains, coverage)
    total = beam_pass(coverage, gains, rounded).reshape(shape)
    rounded, flat0 = second_pass(coverage, omega, gains, total)
    total = beam_pass(coverage, gains, rounded).reshape(shape)
    flat, gram = third_pass(total, flat0)
    basis, factor = finish(gram, flat)
    return basis.reshape(sketch.shape), factor


def solution(mesh):
    return jax.shard_map(
        local,
        mesh=mesh,
        in_specs=(P("beam", "pix", None), P("pix", "beam", None, None), P("pix", "beam")),
        out_specs=(P("beam", "pix", None), P()),
        check_vma=False,
    )
```

time: 228 us -> 228 us (level)
    pallas_call x2 -> x3, Pallas kernels: 188 us -> 177 us  [the longest x1 72.9 us: first_pass(): pl.pallas_call(first_kernel, out_shape=(jax.ShapeDtypeStruct((64, 128, W)...]
    pallas_call x1 -> x2, Pallas kernels: 22.4 us -> 30.6 us  [beam_pass(): pl.pallas_call(beam_kernel, grid_spec=spec, out_shape=jax.ShapeDtypeStruc...]
where the time goes in v5:
time: 228 us
  Pallas kernels  221 us (97%)
  local copies, waits for them, and re-layouts  6.15 us (3%)
    pallas_call x1, Pallas kernels, first_pass(): pl.pallas_call(first_kernel, out_shape=(jax.ShapeDtypeStruct((64, 128, W)...  72.9 us
    pallas_call x1, Pallas kernels, third_pass(): pl.pallas_call(third_kernel, out_shape=(jax.ShapeDtypeStruct((512, 256),...  53.3 us
    pallas_call x1, Pallas kernels, second_pass(): pl.pallas_call(second_kernel, out_shape=(jax.ShapeDtypeStruct((64, 128, W...  51.1 us
    pallas_call x2, Pallas kernels, beam_pass(): pl.pallas_call(beam_kernel, grid_spec=spec, out_shape=jax.ShapeDtypeStruc...  30.6 us
    pallas_call x1, Pallas kernels, finish(): pl.pallas_call(finish_kernel, out_shape=(jax.ShapeDtypeStruct((512, 256),...  12.8 us

profile of v5, /device:TPU:1, one launch (start us, length us, event | category | flops | bytes accessed | tf_op | source)
XLA Modules:
  0.0 227.5 jit_solution(10340037244770178219)
XLA Ops:
  0.6 0.8 copy.5
  1.4 0.7 reshape.22.cov
  2.1 1.1 reshape.23
  3.1 0.7 copy.8
  3.9 72.9 %first_pass.1 = (bf16[64,128,128]{2,1,0:T(8,128)(2,1)}, bf16[128,128,128]{2,1,0:T(8,128)(2,1)}) custom-call(s32[512]{0:T(512)} %reshape.22.cov, bf16[2,512,128]{2,1,0:T(8,128)(2,1)} %bitcast.7, bf16[64,8,128,128]{3,2,1,0:T(8,128)(2,1)} %g.3), custom_call_target="tpu_custom_call" | custom-call | flops 4400000000 | bytes 24000000 | tf_op jit(solution)/shard_map/first_pass/pallas_call | solution.py:347
  76.7 15.3 %beam_pass.2 = f32[16,2,512,128]{3,2,1,0:T(8,128)} custom-call(s32[512]{0:T(512)} %reshape.22.cov, bf16[64,8,128,128]{3,2,1,0:T(8,128)(2,1)} %g.3, bf16[64,128,128]{2,1,0:T(8,128)(2,1)} %get-tuple-element.11.zb), custom_call_target="tpu_custom_call" | custom-call | flops 4300000256 | bytes 38000000 | tf_op jit(solution)/shard_map/beam_pass/pallas_call | solution.py:431
  92.0 51.1 %second_pass.1 = (bf16[64,128,128]{2,1,0:T(8,128)(2,1)}, f32[512,128]{1,0:T(8,128)}) custom-call(s32[512]{0:T(512)} %reshape.22.cov, bf16[128,128,128]{2,1,0:T(8,128)(2,1)} %get-tuple-element.10.om_in, bf16[64,8,128,128]{3,2,1,0:T(8,128)(2,1)} %g.3, f32[4,4,2,512,128]{4,3,2,1,0:T(8,128)} %bitcast.6), custom_call_target="tpu_custom_call" | custom-call | flops 2200000000 | bytes 32000000 | tf_op jit(solution)/shard_map/second_pass/pallas_call | solution.py:612
  143.2 15.3 %beam_pass.3 = f32[16,2,512,128]{3,2,1,0:T(8,128)} custom-call(s32[512]{0:T(512)} %reshape.22.cov, bf16[64,8,128,128]{3,2,1,0:T(8,128)(2,1)} %g.3, bf16[64,128,128]{2,1,0:T(8,128)(2,1)} %get-tuple-element.12.zb), custom_call_target="tpu_custom_call" | custom-call | flops 4300000256 | bytes 38000000 | tf_op jit(solution)/shard_map/beam_pass/pallas_call | solution.py:431
  158.4 53.3 %third_pass.1 = (f32[512,256]{1,0:T(8,128)}, f32[256,256]{1,0:T(8,128)}) custom-call(f32[4,4,2,512,128]{4,3,2,1,0:T(8,128)} %bitcast.5, f32[512,128]{1,0:T(8,128)} %get-tuple-element.13.flat0), custom_call_target="tpu_custom_call" | custom-call | flops 500000000 | bytes 9000000 | tf_op jit(solution)/shard_map/third_pass/pallas_call | solution.py:708
  211.8 0.0 copy-start
  211.8 1.0 copy-done
  212.8 0.0 copy-start.1
  212.8 0.9 copy-done.1
  213.8 12.8 %finish.1 = (f32[512,256]{1,0:T(8,128)S(1)}, f32[256,256]{1,0:T(8,128)}) custom-call(f32[256,256]{1,0:T(8,128)S(1)} %copy-done.1, f32[512,256]{1,0:T(8,128)S(1)} %copy-done), custom_call_target="tpu_custom_call" | custom-call | tf_op jit(solution)/shard_map/finish/pallas_call | solution.py:806
  226.6 0.9 reshape.26
Async XLA Ops:
  211.8 1.0 copy-start
  212.8 0.9 copy-start.1

commit v6 on v5

--- a/solution.py
+++ b/solution.py
@@ -60,9 +60,8 @@
 
 
 W = 128
-CHUNKS = 4
-TC = 64 // CHUNKS
-PART = TC // 8
+CHUNKS1 = 4
+CHUNKS2 = 2
 
 
 def gatherer(sk, raw, gsend, grecv, local):
@@ -162,7 +161,9 @@
             om[pl.ds(4 * q, 4), pl.ds(64 * g, 64), :] = turned.reshape(4, 64, W)
 
 
-def pixel_sums(cov, om, gains, out, gbuf, zf, zs, zb, got, csend, bsend, brecv, local):
+def pixel_sums(chunks, cov, om, gains, out, gbuf, zf, zs, zb, got, csend, bsend, brecv, local):
+    tiles = 64 // chunks
+    half = tiles // 8
     y = lax.axis_index("beam")
     near = neighbours()
     c0, c1, c2, c3 = y, step4(y, 1), step4(y, 2), step4(y, 3)
@@ -174,13 +175,13 @@
         )
 
     def lo(i, c):
-        return pl.ds(TC * i + 2 * PART * c, PART)
+        return pl.ds(tiles * i + 2 * half * c, half)
 
     def hi(i, c):
-        return pl.ds(TC * i + 2 * PART * c + PART, PART)
+        return pl.ds(tiles * i + 2 * half * c + half, half)
 
     def copies(i):
-        own = zb.at[pl.ds(TC * i + 2 * PART * c0, 2 * PART)]
+        own = zb.at[pl.ds(tiles * i + 2 * half * c0, 2 * half)]
         left = zb.at[lo(i, c3)]
         right = zb.at[hi(i, c1)]
         table = (
@@ -198,19 +199,19 @@
         return lambda k: rc(k, i, *table[k])
 
     def store(i):
-        at = pl.ds(TC * i, TC)
-        return pltpu.make_async_copy(zb.at[at], out.at[at], local.at[CHUNKS + i])
+        at = pl.ds(tiles * i, tiles)
+        return pltpu.make_async_copy(zb.at[at], out.at[at], local.at[chunks + i])
 
     def load(i):
-        at = pl.ds(TC * i, TC)
+        at = pl.ds(tiles * i, tiles)
         return pltpu.make_async_copy(gains.at[at], gbuf.at[at], local.at[i])
 
     def begin(i):
         load(i).wait()
 
-        @pl.loop(0, TC, unroll=4)
+        @pl.loop(0, tiles, unroll=4)
         def _(tt):
-            t = i * TC + tt
+            t = i * tiles + tt
             lhs = jnp.concatenate([gbuf[t, s] for s in range(8)], axis=1)
             rhs = jnp.concatenate([om[cov[t * 8 + s]] for s in range(8)], axis=0)
             acc = jnp.dot(lhs, rhs, preferred_element_type=F32)
@@ -263,7 +264,7 @@
         store(i).wait()
 
     def start_loads():
-        for i in range(CHUNKS):
+        for i in range(chunks):
             load(i).start()
 
     return start_loads, (begin, second, third, fourth, fifth, sixth)
@@ -277,17 +278,18 @@
             work(tau - after - n)
 
 
-PIXEL_SCRATCH = [
-    pltpu.VMEM((64, 8, 128, 128), BF),
-    pltpu.VMEM((64, 128, W), F32),
-    pltpu.VMEM((64, 128, W), BF),
-    pltpu.VMEM((64, 128, W), BF),
-    pltpu.VMEM((6, CHUNKS, PART, 128, W), BF),
-    pltpu.VMEM((2, CHUNKS, PART, 128, W), BF),
-    pltpu.SemaphoreType.DMA((10, CHUNKS)),
-    pltpu.SemaphoreType.DMA((10, CHUNKS)),
-    pltpu.SemaphoreType.DMA((2 * CHUNKS,)),
-]
+def pixel_scratch(chunks):
+    return [
+        pltpu.VMEM((64, 8, 128, 128), BF),
+        pltpu.VMEM((64, 128, W), F32),
+        pltpu.VMEM((64, 128, W), BF),
+        pltpu.VMEM((64, 128, W), BF),
+        pltpu.VMEM((6, chunks, 8 // chunks, 128, W), BF),
+        pltpu.VMEM((2, chunks, 8 // chunks, 128, W), BF),
+        pltpu.SemaphoreType.DMA((10, chunks)),
+        pltpu.SemaphoreType.DMA((10, chunks)),
+        pltpu.SemaphoreType.DMA((2 * chunks,)),
+    ]
 
 
 def first_kernel(cov, sk, gains, out, om_out, raw, om, gsend, grecv, local, *rest):
@@ -296,7 +298,7 @@
         gatherer(sk.at[h], raw.at[h], gsend.at[h], grecv.at[h], local.at[h])
         for h in range(2)
     ]
-    start_loads, stages = pixel_sums(cov, om.at[0], gains, out, *rest)
+    start_loads, stages = pixel_sums(CHUNKS1, cov, om.at[0], gains, out, *rest)
     parts[0][0]().start()
     parts[1][0]().start()
     greet(("xr", "xl", "zr", "zl", "sib", "yr", "yl"), near)
@@ -312,9 +314,9 @@
     def keep():
         return pltpu.make_async_copy(om.at[1], om_out, local.at[2])
 
-    @pl.loop(0, CHUNKS + 5)
+    @pl.loop(0, CHUNKS1 + 5)
     def _(tau):
-        run_stages(tau, stages, CHUNKS)
+        run_stages(tau, stages, CHUNKS1)
         for step, at in zip(later[1:], GATHER_AT):
 
             @pl.when(tau == at)
@@ -341,7 +343,7 @@
         pltpu.SemaphoreType.DMA((2, 24)),
         pltpu.SemaphoreType.DMA((2, 24)),
         pltpu.SemaphoreType.DMA((3,)),
-        *PIXEL_SCRATCH,
+        *pixel_scratch(CHUNKS1),
     ]
     hbm = pl.BlockSpec(memory_space=pl.ANY)
     return pl.pallas_call(
@@ -375,7 +377,7 @@
         def _(b):
             acc[b] = jnp.zeros((128, W), F32)
 
-    @pl.loop(0, TILES_STEP, unroll=4)
+    @pl.loop(0, TILES_STEP, unroll=8)
     def _(tt):
         rows = zb[tt]
         for s in range(8):
@@ -439,7 +441,7 @@
         name="beam_pass",
     )(coverage.reshape(-1), gains, rounded)
 
-SUB = 4
+SUB = 2
 ROWS = 256 // SUB
 HALF = ROWS // 2
 
@@ -587,8 +589,8 @@
 
 def second_kernel(cov, om_in, gains, part, out, flat, om, local, *rest):
     near = neighbours()
-    n = len(PIXEL_SCRATCH)
-    start_gains, pixel = pixel_sums(cov, om, gains, out, *rest[:n])
+    n = len(pixel_scratch(CHUNKS2))
+    start_gains, pixel = pixel_sums(CHUNKS2, cov, om, gains, out, *rest[:n])
     start_own, start_swaps, rows = row_sums(
         part, flat, slice(None), *rest[n:]
     )
@@ -600,10 +602,10 @@
     start_swaps()
     fetch.wait()
 
-    @pl.loop(0, max(CHUNKS, SUB) + 5)
+    @pl.loop(0, max(CHUNKS2, SUB) + 5)
     def _(tau):
         for n in range(6):
-            run_stages(tau, pixel[n : n + 1], CHUNKS, n)
+            run_stages(tau, pixel[n : n + 1], CHUNKS2, n)
             run_stages(tau, rows[n : n + 1], SUB, n)
 
 
@@ -620,7 +622,7 @@
         scratch_shapes=[
             pltpu.VMEM((128, 128, W), BF),
             pltpu.SemaphoreType.DMA,
-            *PIXEL_SCRATCH,
+            *pixel_scratch(CHUNKS2),
             *SUM_SCRATCH,
         ],
         compiler_params=pltpu.CompilerParams(

time: 228 us -> 224 us (0.982)
  Pallas kernels: 221 us -> 216 us
where the time goes in v6:
time: 224 us; the launch traced here: 223 us
  Pallas kernels  216 us (96%)
  local copies, waits for them, and re-layouts  6.15 us (3%)
    pallas_call x1, Pallas kernels, first_pass(): pl.pallas_call(first_kernel, out_shape=(jax.ShapeDtypeStruct((64, 128, W)...  72.9 us
    pallas_call x1, Pallas kernels, third_pass(): pl.pallas_call(third_kernel, out_shape=(jax.ShapeDtypeStruct((512, 256),...  52.2 us
    pallas_call x1, Pallas kernels, second_pass(): pl.pallas_call(second_kernel, out_shape=(jax.ShapeDtypeStruct((64, 128, W...  50.3 us
    pallas_call x2, Pallas kernels, beam_pass(): pl.pallas_call(beam_kernel, grid_spec=spec, out_shape=jax.ShapeDtypeStruc...  28.4 us
    pallas_call x1, Pallas kernels, finish(): pl.pallas_call(finish_kernel, out_shape=(jax.ShapeDtypeStruct((512, 256),...  12.8 us

profile of v6, /device:TPU:1, one launch (start us, length us, event | category | flops | bytes accessed | tf_op | source)
XLA Modules:
  0.0 223.3 jit_solution(15405825597973735292)
XLA Ops:
  0.6 0.8 copy.5
  1.4 0.7 reshape.22.cov
  2.1 1.1 reshape.23
  3.1 0.7 copy.8
  3.9 72.9 %first_pass.1 = (bf16[64,128,128]{2,1,0:T(8,128)(2,1)}, bf16[128,128,128]{2,1,0:T(8,128)(2,1)}) custom-call(s32[512]{0:T(512)} %reshape.22.cov, bf16[2,512,128]{2,1,0:T(8,128)(2,1)} %bitcast.7, bf16[64,8,128,128]{3,2,1,0:T(8,128)(2,1)} %g.3), custom_call_target="tpu_custom_call" | custom-call | flops 4400000000 | bytes 24000000 | tf_op jit(solution)/shard_map/first_pass/pallas_call | solution.py:349
  76.7 14.2 %beam_pass.2 = f32[16,2,512,128]{3,2,1,0:T(8,128)} custom-call(s32[512]{0:T(512)} %reshape.22.cov, bf16[64,8,128,128]{3,2,1,0:T(8,128)(2,1)} %g.3, bf16[64,128,128]{2,1,0:T(8,128)(2,1)} %get-tuple-element.11.zb), custom_call_target="tpu_custom_call" | custom-call | flops 4300000256 | bytes 38000000 | tf_op jit(solution)/shard_map/beam_pass/pallas_call | solution.py:433
  90.9 50.3 %second_pass.1 = (bf16[64,128,128]{2,1,0:T(8,128)(2,1)}, f32[512,128]{1,0:T(8,128)}) custom-call(s32[512]{0:T(512)} %reshape.22.cov, bf16[128,128,128]{2,1,0:T(8,128)(2,1)} %get-tuple-element.10.om_in, bf16[64,8,128,128]{3,2,1,0:T(8,128)(2,1)} %g.3, f32[4,4,2,512,128]{4,3,2,1,0:T(8,128)} %bitcast.6), custom_call_target="tpu_custom_call" | custom-call | flops 2200000000 | bytes 32000000 | tf_op jit(solution)/shard_map/second_pass/pallas_call | solution.py:614
  141.2 14.2 %beam_pass.3 = f32[16,2,512,128]{3,2,1,0:T(8,128)} custom-call(s32[512]{0:T(512)} %reshape.22.cov, bf16[64,8,128,128]{3,2,1,0:T(8,128)(2,1)} %g.3, bf16[64,128,128]{2,1,0:T(8,128)(2,1)} %get-tuple-element.12.zb), custom_call_target="tpu_custom_call" | custom-call | flops 4300000256 | bytes 38000000 | tf_op jit(solution)/shard_map/beam_pass/pallas_call | solution.py:433
  155.4 52.2 %third_pass.1 = (f32[512,256]{1,0:T(8,128)}, f32[256,256]{1,0:T(8,128)}) custom-call(f32[4,4,2,512,128]{4,3,2,1,0:T(8,128)} %bitcast.5, f32[512,128]{1,0:T(8,128)} %get-tuple-element.13.flat0), custom_call_target="tpu_custom_call" | custom-call | flops 500000000 | bytes 9000000 | tf_op jit(solution)/shard_map/third_pass/pallas_call | solution.py:710
  207.6 0.0 copy-start
  207.6 1.0 copy-done
  208.7 0.0 copy-start.1
  208.7 0.9 copy-done.1
  209.6 12.8 %finish.1 = (f32[512,256]{1,0:T(8,128)S(1)}, f32[256,256]{1,0:T(8,128)}) custom-call(f32[256,256]{1,0:T(8,128)S(1)} %copy-done.1, f32[512,256]{1,0:T(8,128)S(1)} %copy-done), custom_call_target="tpu_custom_call" | custom-call | tf_op jit(solution)/shard_map/finish/pallas_call | solution.py:808
  222.4 0.9 reshape.26
Async XLA Ops:
  207.6 1.0 copy-start
  208.7 0.9 copy-start.1

commit v7 on v6

--- a/solution.py
+++ b/solution.py
@@ -377,7 +377,7 @@
         def _(b):
             acc[b] = jnp.zeros((128, W), F32)
 
-    @pl.loop(0, TILES_STEP, unroll=8)
+    @pl.loop(0, TILES_STEP, unroll=16)
     def _(tt):
         rows = zb[tt]
         for s in range(8):

time: 224 us -> 223 us (level)
  no operation moved by 1% of the time
where the time goes in v7:
time: 223 us; the launch traced here: 222 us
  Pallas kernels  215 us (96%)
  local copies, waits for them, and re-layouts  6.15 us (3%)
    pallas_call x1, Pallas kernels, first_pass(): pl.pallas_call(first_kernel, out_shape=(jax.ShapeDtypeStruct((64, 128, W)...  72.9 us
    pallas_call x1, Pallas kernels, third_pass(): pl.pallas_call(third_kernel, out_shape=(jax.ShapeDtypeStruct((512, 256),...  52.1 us
    pallas_call x1, Pallas kernels, second_pass(): pl.pallas_call(second_kernel, out_shape=(jax.ShapeDtypeStruct((64, 128, W...  50.3 us
    pallas_call x2, Pallas kernels, beam_pass(): pl.pallas_call(beam_kernel, grid_spec=spec, out_shape=jax.ShapeDtypeStruc...  27.2 us
    pallas_call x1, Pallas kernels, finish(): pl.pallas_call(finish_kernel, out_shape=(jax.ShapeDtypeStruct((512, 256),...  12.8 us

profile of v7, /device:TPU:1, one launch (start us, length us, event | category | flops | bytes accessed | tf_op | source)
XLA Modules:
  0.0 222.2 jit_solution(193018186279068806)
XLA Ops:
  0.6 0.8 copy.5
  1.4 0.7 reshape.22.cov
  2.1 1.1 reshape.23
  3.1 0.7 copy.8
  3.9 72.9 %first_pass.1 = (bf16[64,128,128]{2,1,0:T(8,128)(2,1)}, bf16[128,128,128]{2,1,0:T(8,128)(2,1)}) custom-call(s32[512]{0:T(512)} %reshape.22.cov, bf16[2,512,128]{2,1,0:T(8,128)(2,1)} %bitcast.7, bf16[64,8,128,128]{3,2,1,0:T(8,128)(2,1)} %g.3), custom_call_target="tpu_custom_call" | custom-call | flops 4400000000 | bytes 24000000 | tf_op jit(solution)/shard_map/first_pass/pallas_call | solution.py:349
  76.7 13.6 %beam_pass.2 = f32[16,2,512,128]{3,2,1,0:T(8,128)} custom-call(s32[512]{0:T(512)} %reshape.22.cov, bf16[64,8,128,128]{3,2,1,0:T(8,128)(2,1)} %g.3, bf16[64,128,128]{2,1,0:T(8,128)(2,1)} %get-tuple-element.11.zb), custom_call_target="tpu_custom_call" | custom-call | flops 4300000256 | bytes 38000000 | tf_op jit(solution)/shard_map/beam_pass/pallas_call | solution.py:433
  90.3 50.3 %second_pass.1 = (bf16[64,128,128]{2,1,0:T(8,128)(2,1)}, f32[512,128]{1,0:T(8,128)}) custom-call(s32[512]{0:T(512)} %reshape.22.cov, bf16[128,128,128]{2,1,0:T(8,128)(2,1)} %get-tuple-element.10.om_in, bf16[64,8,128,128]{3,2,1,0:T(8,128)(2,1)} %g.3, f32[4,4,2,512,128]{4,3,2,1,0:T(8,128)} %bitcast.6), custom_call_target="tpu_custom_call" | custom-call | flops 2200000000 | bytes 32000000 | tf_op jit(solution)/shard_map/second_pass/pallas_call | solution.py:614
  140.7 13.6 %beam_pass.3 = f32[16,2,512,128]{3,2,1,0:T(8,128)} custom-call(s32[512]{0:T(512)} %reshape.22.cov, bf16[64,8,128,128]{3,2,1,0:T(8,128)(2,1)} %g.3, bf16[64,128,128]{2,1,0:T(8,128)(2,1)} %get-tuple-element.12.zb), custom_call_target="tpu_custom_call" | custom-call | flops 4300000256 | bytes 38000000 | tf_op jit(solution)/shard_map/beam_pass/pallas_call | solution.py:433
  154.3 52.1 %third_pass.1 = (f32[512,256]{1,0:T(8,128)}, f32[256,256]{1,0:T(8,128)}) custom-call(f32[4,4,2,512,128]{4,3,2,1,0:T(8,128)} %bitcast.5, f32[512,128]{1,0:T(8,128)} %get-tuple-element.13.flat0), custom_call_target="tpu_custom_call" | custom-call | flops 500000000 | bytes 9000000 | tf_op jit(solution)/shard_map/third_pass/pallas_call | solution.py:710
  206.4 0.0 copy-start
  206.4 1.0 copy-done
  207.5 0.0 copy-start.1
  207.5 0.9 copy-done.1
  208.4 12.8 %finish.1 = (f32[512,256]{1,0:T(8,128)S(1)}, f32[256,256]{1,0:T(8,128)}) custom-call(f32[256,256]{1,0:T(8,128)S(1)} %copy-done.1, f32[512,256]{1,0:T(8,128)S(1)} %copy-done), custom_call_target="tpu_custom_call" | custom-call | tf_op jit(solution)/shard_map/finish/pallas_call | solution.py:808
  221.2 0.9 reshape.26
Async XLA Ops:
  206.4 1.0 copy-start
  207.5 0.9 copy-start.1
